TPU v7x, 512 devices: a whole 4x8x8 slice. The times are simulated.
512 devices in a mesh: dp: 32 (over z, x_lo, core), head: 16 (over x_hi, y).
Axes of the slice: x: 4 (x_hi: 2, x_lo: 2; x = x_hi * 2 + x_lo), y: 8, z: 8, core: 2. Of those that a mesh axis runs over, the one named last changes fastest.
Arguments:
- stream: bfloat16 [128, 8192], P('head', 'dp'), may hold values from -32.7 to 32.7
- state: float32 [128, 128, 8192], P('dp', 'head'), may hold values from -6 to 6
- mixer_norm_gain: bfloat16 [8192], P('dp'), may hold values from 0.5 to 1.5
- head_input_weight: bfloat16 [8192, 8192], P('dp', 'head'), may hold values from -0.0625 to 0.0625
- output_gate_weight: bfloat16 [8192, 8192], P('dp', 'head'), may hold values from -0.0625 to 0.0625
- group_map_weight: bfloat16 [8192, 2048], P('dp', 'head'), may hold values from -0.0625 to 0.0625
- step_size_weight: bfloat16 [8192, 128], P('dp', 'head'), may hold values from -0.0625 to 0.0625
- step_size_bias: float32 [128], P('head'), may hold values from -3 to 0.5
- head_decay_rate: float32 [128], P('head'), may hold values from 0.5 to 16
- head_skip_gain: float32 [128], P('head'), may hold values from 0.5 to 2
- gate_norm_gain: bfloat16 [8192], P('head'), may hold values from 0.5 to 1.5
- mixer_output_weight: bfloat16 [8192, 8192], P('head', 'dp'), may hold values from -0.0625 to 0.0625
- adapter_input_down: bfloat16 [8, 8192, 16], P(None, 'dp'), may hold values from -0.0625 to 0.0625
- adapter_input_up: bfloat16 [8, 16, 2, 8192], P(None, None, None, 'head'), may hold values from -1.5 to 1.5
- adapter_output_down: bfloat16 [8, 8192, 16], P(None, 'head'), may hold values from -0.0625 to 0.0625
- adapter_output_up: bfloat16 [8, 16, 8192], P(None, None, 'dp'), may hold values from -1.5 to 1.5
- mlp_norm_gain: bfloat16 [8192], P('dp'), may hold values from 0.5 to 1.5
- mlp_up_weight: bfloat16 [8192, 16384], P('dp', 'head'), may hold values from -0.0625 to 0.0625
- mlp_down_weight: bfloat16 [16384, 8192], P('head', 'dp'), may hold values from -0.046875 to 0.046875
- slot_adapter_index: int32 [128], P('dp'), may hold values from 0 to 8, as said below
- segment_first_slot: int32 [8], replicated, may hold values from 0 to 124, as said below
Outputs:
- out_stream: bfloat16 [128, 8192], P('head', 'dp')
- new_state: float32 [128, 128, 8192], P('dp', 'head')
Inputs may be any that keep to these rules, and one draw needn't show every extreme that they name: `slot_adapter_index`: row slots form 8 segments, one for each adapter in order of adapter number; each is one or more whole tiles of 4 slots, the last segment exactly one tile; its live rows come first and carry its adapter number, the rest carry 8; each segment has at least one live row and at least one padding slot. `segment_first_slot`: the first slot of each segment described with slot_adapter_index: strictly increasing multiples of 4, the first 0, the last 124.
All inputs are finite; a program needn't handle non-finite values.
Results may differ from a plain program's by a relative error of at most 0.033.
Values may be sent and summed in bfloat16 or wider, within the bound.
No kernel may reach another device: no remote copies, remote signals or barrier semaphores. Data moves between devices by JAX's collectives and lax.ppermute only.
A program may use at most 64 MiB of HBM per device.

v0:
```python
import jax
import jax.numpy as jnp
from jax import lax
from jax.sharding import PartitionSpec as P

MODEL_WIDTH = 8192
HEAD_TOTAL = 128
HEAD_CHANNELS = 64
NSTATE = 128
GROUPS = 8
ADAPTER_RANK = 16
ADAPTER_COUNT = 8
TILE = 4


highest_precision = lax.Precision.HIGHEST
eps = 1e-05


def per_device(
    stream,
    state,
    mixer_norm_gain,
    head_input_weight,
    output_gate_weight,
    group_map_weight,
    step_size_weight,
    step_size_bias,
    head_decay_rate,
    head_skip_gain,
    gate_norm_gain,
    mixer_output_weight,
    adapter_input_down,
    adapter_input_up,
    adapter_output_down,
    adapter_output_up,
    mlp_norm_gain,
    mlp_up_weight,
    mlp_down_weight,
    slot_adapter_index,
    segment_first_slot,
):
    dp_count = lax.axis_size("dp")
    head_count = lax.axis_size("head")
    head_index = lax.axis_index("head")
    dp_index = lax.axis_index("dp")
    own_rows = state.shape[0]
    heads_here = state.shape[1]
    all_rows = own_rows * dp_count
    rows_head = all_rows // head_count
    local_width = stream.shape[1]
    local_inner_width = heads_here * HEAD_CHANNELS
    group_cols = group_map_weight.shape[1]
    lane_groups = ADAPTER_COUNT * ADAPTER_RANK
    gathered = lax.all_gather(stream, "head", axis=0, tiled=True)
    gathered_wide = gathered.astype(jnp.float32)
    mix_squares = lax.psum(jnp.sum(gathered_wide * gathered_wide, axis=1), "dp")
    mix_scale = lax.rsqrt(mix_squares / MODEL_WIDTH + eps)
    normed = (
        gathered_wide * mix_scale[:, None] * mixer_norm_gain.astype(jnp.float32)[None, :]
    ).astype(jnp.bfloat16)
    tile_starts = jnp.arange(all_rows // TILE, dtype=jnp.int32) * TILE
    tile_adapter = (
        jnp.sum((segment_first_slot[None, :] <= tile_starts[:, None]).astype(jnp.int32), axis=1) - 1
    )
    row_adapter = jnp.repeat(tile_adapter, TILE)
    adapter_pick = (
        row_adapter[:, None] == jnp.arange(ADAPTER_COUNT, dtype=jnp.int32)[None, :]
    ).astype(jnp.float32)
    input_table = jnp.transpose(adapter_input_down, (1, 0, 2)).reshape(local_width, lane_groups)
    joined_weight = jnp.concatenate(
        [head_input_weight, output_gate_weight, group_map_weight, step_size_weight], axis=1
    )
    main_term = jnp.dot(normed, joined_weight, preferred_element_type=jnp.float32)
    lane_term = jnp.dot(normed, input_table, preferred_element_type=jnp.float32).reshape(
        own_rows * lax.axis_size("dp"), ADAPTER_COUNT, ADAPTER_RANK
    )
    chosen = adapter_pick
    low_term = jnp.sum(lane_term * chosen[:, :, None], axis=1)
    projected = lax.psum_scatter(
        jnp.concatenate([main_term, low_term], axis=1), "dp", scatter_dimension=0, tiled=True
    )
    split_group = 2 * local_inner_width
    split_step = split_group + group_cols
    split_low = split_step + heads_here
    own_pick = lax.dynamic_slice_in_dim(adapter_pick, dp_index * own_rows, own_rows, 0)
    low_rank = projected[:, split_low:]
    spread_lowrank = (own_pick[:, :, None] * low_rank[:, None, :]).reshape(own_rows, lane_groups)
    input_lift = jnp.dot(
        spread_lowrank,
        adapter_input_up.astype(jnp.float32).reshape(lane_groups, 2 * local_inner_width),
        precision=highest_precision,
    )
    x_part = projected[:, :local_inner_width] + input_lift[:, :local_inner_width]
    z_part = projected[:, local_inner_width:split_group] + input_lift[:, local_inner_width:]
    group_part = projected[:, split_group:split_step]
    step_raw = projected[:, split_step:split_low]
    group_all = lax.all_gather(group_part, "head", axis=1, tiled=True)
    input_mat = jax.nn.silu(group_all[:, : GROUPS * NSTATE]).reshape(own_rows, GROUPS, NSTATE)
    output_mat = jax.nn.silu(group_all[:, GROUPS * NSTATE :]).reshape(own_rows, GROUPS, NSTATE)
    global_head = head_index * heads_here + jnp.arange(heads_here, dtype=jnp.int32)
    head_group = (
        global_head[:, None] // (HEAD_TOTAL // GROUPS)
        == jnp.arange(GROUPS, dtype=jnp.int32)[None, :]
    ).astype(jnp.float32)
    head_input = jnp.einsum("rgn,hg->rhn", input_mat, head_group, precision=highest_precision)
    head_output = jnp.einsum("rgn,hg->rhn", output_mat, head_group, precision=highest_precision)
    step_size = jax.nn.softplus(step_raw + step_size_bias[None, :])
    forget = jnp.exp(-step_size * head_decay_rate[None, :])
    x_heads = jax.nn.silu(x_part).reshape(own_rows, heads_here, HEAD_CHANNELS)
    old_state = state.reshape(own_rows, heads_here, HEAD_CHANNELS, NSTATE)
    fresh = (
        forget[:, :, None, None] * old_state
        + (step_size[:, :, None] * x_heads)[:, :, :, None] * head_input[:, :, None, :]
    )
    live_rows = slot_adapter_index < ADAPTER_COUNT
    new_state = jnp.where(live_rows[:, None, None, None], fresh, old_state).reshape(state.shape)
    read_out = (
        jnp.sum(fresh * head_output[:, :, None, :], axis=3)
        + head_skip_gain[None, :, None] * x_heads
    )
    gated = read_out.reshape(own_rows, local_inner_width) * jax.nn.silu(z_part)
    gated_heads = gated.reshape(own_rows, heads_here, HEAD_CHANNELS)
    head_squares = jnp.sum(gated_heads * gated_heads, axis=2)
    group_squares = lax.psum(jnp.dot(head_squares, head_group, precision=highest_precision), "head")
    head_scale = lax.rsqrt(
        jnp.dot(group_squares, head_group.T, precision=highest_precision)
        / (HEAD_TOTAL * HEAD_CHANNELS // GROUPS)
        + eps
    )
    normed_gate = (gated_heads * head_scale[:, :, None]).reshape(
        own_rows, local_inner_width
    ) * gate_norm_gain.astype(jnp.float32)[None, :]
    mixed_in = jnp.where(live_rows[:, None], normed_gate, 0.0).astype(jnp.bfloat16)
    output_table = jnp.transpose(adapter_output_down, (1, 0, 2)).reshape(
        local_inner_width, lane_groups
    )
    output_lift = adapter_output_up.astype(jnp.float32).reshape(lane_groups, local_width)
    shard_rows = lax.all_gather(mixed_in, "dp", axis=0, tiled=True)
    row_count = shard_rows.shape[0]
    main_term = jnp.dot(shard_rows, mixer_output_weight, preferred_element_type=jnp.float32)
    lane_term = jnp.dot(shard_rows, output_table, preferred_element_type=jnp.float32).reshape(
        row_count, ADAPTER_COUNT, ADAPTER_RANK
    )
    chosen = adapter_pick
    spread = (lane_term * chosen[:, :, None]).reshape(row_count, lane_groups)
    mixer_terms = main_term + jnp.dot(spread, output_lift, precision=highest_precision)
    mixer_all = lax.psum(mixer_terms, "head")
    resid_all = (gathered_wide + mixer_all).astype(jnp.bfloat16)
    resid_wide = resid_all.astype(jnp.float32)
    all_squares = lax.psum(jnp.sum(resid_wide * resid_wide, axis=1), "dp")
    all_scale = lax.rsqrt(all_squares / MODEL_WIDTH + eps)
    normed_mlp = (
        resid_wide * all_scale[:, None] * mlp_norm_gain.astype(jnp.float32)[None, :]
    ).astype(jnp.bfloat16)
    resid_rows = lax.dynamic_slice_in_dim(resid_all, head_index * rows_head, rows_head, 0)
    up_all = lax.psum(
        jnp.dot(normed_mlp, mlp_up_weight, preferred_element_type=jnp.float32).astype(jnp.bfloat16),
        "dp",
    ).astype(jnp.float32)
    hidden_all = (jnp.maximum(up_all, 0.0) ** 2).astype(jnp.bfloat16)
    mlp_terms = jnp.dot(hidden_all, mlp_down_weight, preferred_element_type=jnp.float32)
    mlp_rows = lax.psum_scatter(
        mlp_terms.astype(jnp.bfloat16), "head", scatter_dimension=0, tiled=True
    ).astype(jnp.float32)
    out_stream = (resid_rows.astype(jnp.float32) + mlp_rows).astype(jnp.bfloat16)
    return (out_stream, new_state)


def solution(mesh):
    in_specs = (
        P("head", "dp"),
        P("dp", "head", None),
        P("dp"),
        P("dp", "head"),
        P("dp", "head"),
        P("dp", "head"),
        P("dp", "head"),
        P("head"),
        P("head"),
        P("head"),
        P("head"),
        P("head", "dp"),
        P(None, "dp", None),
        P(None, None, None, "head"),
        P(None, "head", None),
        P(None, None, "dp"),
        P("dp"),
        P("dp", "head"),
        P("head", "dp"),
        P("dp"),
        P(),
    )
    out_specs = (P("head", "dp"), P("dp", "head", None))
    return jax.shard_map(
        per_device, mesh=mesh, in_specs=in_specs, out_specs=out_specs, check_vma=False
    )
```

profile of v0, /device:TPU:16, one launch (start us, length us, event | category | flops | bytes accessed | tf_op | source)
XLA Modules:
  0.0 1050.7 jit_solution(8553884326662362820)
XLA Ops:
  7.2 37.4 %all_gather.9 = bf16[128,256]{1,0:T(8,128)(2,1)S(1)} all-gather(bf16[8,256]{1,0:T(8,128)(2,1)} %param.21), channel_id=1, replica_groups=mesh['dp'=32,'head'=16] {'head'}, dimensions={0}, use_global_device_ids=true | all-gather | bytes 69632 | tf_op jit(solution)/shard_map/all_gather | solution.py:55
  44.8 57.8 %psum.35 = f32[128]{0:T(128)S(1)} all-reduce(f32[128]{0:T(128)S(1)} %fusion.19), channel_id=1, replica_groups=mesh['dp'=32,'head'=16] {'dp'}, use_global_device_ids=true, to_apply=%region_1.0 | all-reduce | flops 128 | bytes 1024 | tf_op jit(solution)/shard_map/psum | solution.py:57
  102.6 0.7 convert_reduce_fusion
  103.6 0.7 convert_element_type.62
  104.2 0.8 copy.72
  105.1 1.1 fusion
  106.1 1.5 fusion.7
  107.7 0.9 pad_maximum_fusion
  109.0 1.3 dynamic-slice
  110.9 215.7 %all-reduce.9.cloned.1.call-done = f32[128,1176]{0,1:T(8,128)} async-done(((f32[128,1176]{0,1:T(8,128)}), f32[128,1176]{0,1:T(8,128)}) %all-reduce.9.cloned.1.call-update) | async-done | bytes 602128
  326.6 0.8 dynamic-slice.4
  327.7 1.3 constant_dynamic-slice_fusion.1
  329.1 0.2 fusion.53
  329.4 0.8 multiply_exponential_fusion
  330.5 1.0 dynamic-slice.5
  331.5 36.4 %all_gather.10 = f32[4,2048]{1,0:T(4,128)S(1)} all-gather(f32[4,128]{1,0:T(4,128)S(1)} %copy.88), channel_id=1, replica_groups=mesh['dp'=32,'head'=16] {'head'}, dimensions={1}, use_global_device_ids=true | all-gather | bytes 34816 | tf_op jit(solution)/shard_map/all_gather | solution.py:98
  367.9 0.2 convolution_bitcast_fusion.2
  368.1 0.2 convolution_bitcast_fusion.1
  368.4 0.7 fusion.4
  369.8 36.6 %psum.36 = f32[4,8]{1,0:T(4,128)S(1)} all-reduce(f32[4,8]{1,0:T(4,128)S(1)} %fusion.39), channel_id=1, replica_groups=mesh['dp'=32,'head'=16] {'head'}, use_global_device_ids=true, to_apply=%region_7.8 | all-reduce | flops 32 | bytes 256 | tf_op jit(solution)/shard_map/psum | solution.py:125
  406.9 30.7 %all-gather = bf16[32,4,512]{2,1,0:T(4,128)(2,1)S(1)} all-gather(bf16[1,4,512]{2,1,0:T(4,128)(2,1)S(1)} %fusion.38), channel_id=1, replica_groups=mesh['dp'=32,'head'=16] {'dp'}, dimensions={0}, use_global_device_ids=true | all-gather | bytes 135168 | tf_op jit(solution)/shard_map/all_gather | solution.py:139
  437.9 0.3 convolution_bitcast_fusion
  438.2 0.8 convolution_add_fusion
  439.1 157.0 %all-reduce.5.cloned.1.call-done = f32[128,256]{1,0:T(8,128)} async-done(((f32[128,256]{1,0:T(8,128)}), f32[128,256]{1,0:T(8,128)}) %all-reduce.5.cloned.1.call-update) | async-done | bytes 131088 | tf_op jit(solution)/shard_map/psum | solution.py:148
  596.1 1.0 fusion.16
  597.1 53.0 %psum.38 = f32[128]{0:T(128)S(1)} all-reduce(f32[128]{0:T(128)S(1)} %get-tuple-element.2), channel_id=1, replica_groups=mesh['dp'=32,'head'=16] {'dp'}, use_global_device_ids=true, to_apply=%region_10.11 | all-reduce | flops 128 | bytes 1024 | tf_op jit(solution)/shard_map/psum | solution.py:151
  650.1 1.0 convolution_convert_fusion
  651.2 230.0 %all-reduce.7.cloned.1.call-done = bf16[128,1024]{1,0:T(8,128)(2,1)} async-done(((bf16[128,1024]{1,0:T(8,128)(2,1)}), bf16[128,1024]{1,0:T(8,128)(2,1)}) %all-reduce.7.cloned.1.call-update) | async-done | bytes 262160 | tf_op jit(solution)/shard_map/psum | solution.py:157
  881.1 1.8 convolution_convert_fusion.1
  883.0 1.3 fusion.6
  884.3 158.6 %reduce-scatter.3.cloned.1.call-done = bf16[8,256]{1,0:T(8,128)(2,1)} async-done(((bf16[128,256]{1,0:T(8,128)(2,1)}), bf16[8,256]{1,0:T(8,128)(2,1)}) %reduce-scatter.3.cloned.1.call-update) | async-done | bytes 4112 | tf_op jit(solution)/shard_map/reduce_scatter | solution.py:163
  1042.9 1.3 add_convert_fusion
  (77 shorter events, 3.2 us)
Async XLA Ops:
  7.2 642.9 %copy-start = (bf16[256,1024]{1,0:T(8,128)(2,1)S(1)}, bf16[256,1024]{1,0:T(8,128)(2,1)}, u32[]{:S(2)}) copy-start(bf16[256,1024]{1,0:T(8,128)(2,1)} %param.38) | copy-start | bytes 1572868
  7.2 319.5 %all-reduce.9.cloned.1.call-start = ((), (), s32[]{:S(2)}) async-start(), calls=%async_computation.4 | async-start | bytes 1204224
  107.6 1.2 copy-start.2
  107.6 1.2 copy-start.7
  107.6 1.3 copy-start.6
  107.6 3.3 copy-start.11
  108.5 487.6 %all-reduce.5.cloned.1.call-start = ((), (), s32[]{:S(2)}) async-start(), calls=%async_computation.1 | async-start | bytes 262144 | tf_op jit(solution)/shard_map/psum | solution.py:148
  108.8 220.7 %copy-start.8 = (f32[8]{0:T(128)S(1)}, f32[8]{0:T(128)}, u32[]{:S(2)}) copy-start(f32[8]{0:T(128)} %param.29) | copy-start | bytes 100
  108.8 220.7 %copy-start.9 = (f32[8]{0:T(128)S(1)}, f32[8]{0:T(128)}, u32[]{:S(2)}) copy-start(f32[8]{0:T(128)} %param.28) | copy-start | bytes 100
  327.7 40.8 %copy-start.1 = (f32[4,8,8192]{2,1,0:T(8,128)S(1)}, f32[4,8,8192]{2,1,0:T(8,128)}, u32[]{:S(2)}) copy-start(f32[4,8,8192]{2,1,0:T(8,128)} %param.22) | copy-start | bytes 3145732
  369.1 68.6 %copy-start.4 = (bf16[8,512,16]{1,2,0:T(8,128)(2,1)S(1)}, bf16[8,512,16]{1,2,0:T(8,128)(2,1)}, u32[]{:S(2)}) copy-start(bf16[8,512,16]{1,2,0:T(8,128)(2,1)} %param.35) | copy-start | bytes 393220
  369.2 68.7 %copy-start.5 = (bf16[8,16,256]{2,1,0:T(8,128)(2,1)S(1)}, bf16[8,16,256]{2,1,0:T(8,128)(2,1)}, u32[]{:S(2)}) copy-start(bf16[8,16,256]{2,1,0:T(8,128)(2,1)} %param.36) | copy-start | bytes 196612
  369.4 68.8 %copy-start.3 = (bf16[512,256]{1,0:T(8,128)(2,1)S(1)}, bf16[512,256]{1,0:T(8,128)(2,1)}, u32[]{:S(2)}) copy-start(bf16[512,256]{1,0:T(8,128)(2,1)} %param.32) | copy-start | bytes 786436
  406.7 32.4 %copy-start.12 = (bf16[256]{0:T(256)(128)(2,1)S(1)}, bf16[256]{0:T(256)(128)(2,1)}, u32[]{:S(2)}) copy-start(bf16[256]{0:T(256)(128)(2,1)} %param.37) | copy-start | bytes 1540
  438.2 443.0 %copy-start.10 = (bf16[1024,256]{1,0:T(8,128)(2,1)S(1)}, bf16[1024,256]{1,0:T(8,128)(2,1)}, u32[]{:S(2)}) copy-start(bf16[1024,256]{1,0:T(8,128)(2,1)} %param.39) | copy-start | bytes 1572868
  439.0 442.1 %all-reduce.7.cloned.1.call-start = ((), (), s32[]{:S(2)}) async-start(), calls=%async_computation.2 | async-start | bytes 524288 | tf_op jit(solution)/shard_map/psum | solution.py:157
  651.1 391.8 %reduce-scatter.3.cloned.1.call-start = ((), (), s32[]{:S(2)}) async-start(), calls=%async_computation.3 | async-start | bytes 69632 | tf_op jit(solution)/shard_map/reduce_scatter | solution.py:163
Sparse Core Ops, SparseCore 0:
  108.7 217.9 all-reduce.8
  439.2 156.8 all-reduce.4
  651.2 229.8 all-reduce.6
  885.8 157.0 reduce-scatter.2
where the time goes:
time: 1050 us
  waiting for transfers between devices  761 us (72%)
  blocking collectives  252 us (24%)
  between operations  14.7 us (1%)
    psum x1, waiting for transfers between devices, per_device(): lax.psum(jnp.dot(normed_mlp, mlp_up_weight, preferred_element_type=jnp.fl...  230 us
    unnamed x5, waiting for transfers between devices  216 us
    reduce_scatter x1, waiting for transfers between devices, per_device(): lax.psum_scatter(mlp_terms.astype(jnp.bfloat16), 'head', scatter_dimensio...  159 us
    psum x1, waiting for transfers between devices, per_device(): mixer_all = lax.psum(mixer_terms, 'head')  157 us
    psum x1, blocking collectives, per_device(): mix_squares = lax.psum(jnp.sum(gathered_wide * gathered_wide, axis=1), 'dp')  57.8 us
    psum x1, blocking collectives, per_device(): all_squares = lax.psum(jnp.sum(resid_wide * resid_wide, axis=1), 'dp')  53 us
    all_gather x1, blocking collectives, per_device(): gathered = lax.all_gather(stream, 'head', axis=0, tiled=True)  37.4 us
    psum x1, blocking collectives, per_device(): lax.psum(jnp.dot(head_squares, head_group, precision=highest_precision),...  36.6 us
  transfers between devices with their start and end apart: 4, of which 4 were waited for; matrix products, arithmetic and copies ran while one was open for 0% of the time, Pallas kernels for 0%

commit v1 on v0

v1 whole, which is shorter than its diff:
```python
import jax
import jax.numpy as jnp
from jax import lax
from jax.sharding import PartitionSpec as P

MODEL_WIDTH = 8192
HEAD_TOTAL = 128
HEAD_CHANNELS = 64
NSTATE = 128
GROUPS = 8
ADAPTER_RANK = 16
ADAPTER_COUNT = 8
TILE = 4
LANES = 128

eps = 1e-05
f32 = jnp.float32
bf16 = jnp.bfloat16


def halves(value):
    high = lax.reduce_precision(value, exponent_bits=8, mantissa_bits=7)
    return high.astype(bf16), (value - high).astype(bf16)


def split_dot(value, weight):
    high, low = halves(value)
    rows = value.shape[0]
    both = jnp.dot(jnp.concatenate([high, low], axis=0), weight, preferred_element_type=f32)
    return both[:rows] + both[rows:]


def fill(columns):
    joined = jnp.concatenate(columns, axis=1)
    return jnp.pad(joined, ((0, 0), (0, -joined.shape[1] % LANES)))


def spread_all(block, axis, count):
    copies = jnp.broadcast_to(block[None], (count,) + block.shape)
    return lax.all_to_all(copies, axis, 0, 0)


def trade(blocks, axis, groups=None):
    return lax.all_to_all(blocks, axis, 0, 0, axis_index_groups=groups)


def per_device(
    stream,
    state,
    mixer_norm_gain,
    head_input_weight,
    output_gate_weight,
    group_map_weight,
    step_size_weight,
    step_size_bias,
    head_decay_rate,
    head_skip_gain,
    gate_norm_gain,
    mixer_output_weight,
    adapter_input_down,
    adapter_input_up,
    adapter_output_down,
    adapter_output_up,
    mlp_norm_gain,
    mlp_up_weight,
    mlp_down_weight,
    slot_adapter_index,
    segment_first_slot,
):
    dp_count = lax.axis_size("dp")
    head_count = lax.axis_size("head")
    head_index = lax.axis_index("head")
    dp_index = lax.axis_index("dp")
    own_rows = state.shape[0]
    heads_here = state.shape[1]
    all_rows = own_rows * dp_count
    rows_head = all_rows // head_count
    local_width = stream.shape[1]
    inner = heads_here * HEAD_CHANNELS
    hidden_here = mlp_up_weight.shape[1]
    lane_groups = ADAPTER_COUNT * ADAPTER_RANK
    shares = head_count // GROUPS

    first_move = [(h // shares + (h % shares) * GROUPS, h) for h in range(head_count)]
    second_move = [
        (h // shares + ((h + 1) % shares) * GROUPS, h) for h in range(head_count)
    ]
    first_map = lax.ppermute(group_map_weight, "head", first_move)
    second_map = lax.ppermute(group_map_weight, "head", second_move)

    gathered = spread_all(stream, "head", head_count).reshape(all_rows, local_width)
    wide = gathered.astype(f32)
    gained = (wide * mixer_norm_gain.astype(f32)[None, :]).astype(bf16)
    mix_squares = jnp.sum(wide * wide, axis=1, keepdims=True)

    row_tile = jnp.arange(all_rows, dtype=jnp.int32) // TILE * TILE
    row_adapter = (
        jnp.sum((segment_first_slot[None, :] <= row_tile[:, None]).astype(jnp.int32), axis=1) - 1
    )
    lane_adapter = jnp.arange(lane_groups, dtype=jnp.int32) // ADAPTER_RANK
    lane_pick = row_adapter[:, None] == lane_adapter[None, :]
    input_table = jnp.transpose(adapter_input_down, (1, 0, 2)).reshape(local_width, lane_groups)
    joined = jnp.concatenate(
        [head_input_weight, output_gate_weight, first_map, second_map, input_table], axis=1
    )
    main = jnp.dot(gained, joined, preferred_element_type=f32)
    map_end = 2 * inner + 2 * NSTATE
    low = jnp.where(lane_pick, main[:, map_end:], 0.0).astype(bf16)
    step = jnp.dot(gained, step_size_weight, preferred_element_type=f32)
    step_high, step_low = halves(step)
    squares_high, squares_low = halves(mix_squares)
    sent = jnp.concatenate(
        [main[:, :map_end].astype(bf16), low, fill([step_high, step_low, squares_high, squares_low])],
        axis=1,
    )
    summed = jnp.sum(
        trade(sent.reshape(dp_count, own_rows, sent.shape[1]), "dp").astype(f32), axis=0
    )
    tail = map_end + lane_groups
    squares = summed[:, tail + 2 * heads_here : tail + 2 * heads_here + 1] + summed[
        :, tail + 2 * heads_here + 1 : tail + 2 * heads_here + 2
    ]
    mix_scale = lax.rsqrt(squares / MODEL_WIDTH + eps)
    projected = summed * mix_scale
    low_rank = projected[:, map_end:tail]
    lift = split_dot(low_rank, adapter_input_up.reshape(lane_groups, 2 * inner))
    x_part = projected[:, :inner] + lift[:, :inner]
    z_part = projected[:, inner : 2 * inner] + lift[:, inner:]
    step_raw = (
        projected[:, tail : tail + heads_here]
        + projected[:, tail + heads_here : tail + 2 * heads_here]
    )
    first_part = projected[:, 2 * inner : 2 * inner + NSTATE]
    second_part = projected[:, 2 * inner + NSTATE : map_end]
    input_first = head_index % shares == 0
    input_mat = jax.nn.silu(jnp.where(input_first, first_part, second_part))
    output_mat = jax.nn.silu(jnp.where(input_first, second_part, first_part))

    step_size = jax.nn.softplus(step_raw + step_size_bias[None, :])
    forget = jnp.exp(-step_size * head_decay_rate[None, :])
    x_heads = jax.nn.silu(x_part).reshape(own_rows, heads_here, HEAD_CHANNELS)
    old_state = state.reshape(own_rows, heads_here, HEAD_CHANNELS, NSTATE)
    fresh = (
        forget[:, :, None, None] * old_state
        + (step_size[:, :, None] * x_heads)[:, :, :, None] * input_mat[:, None, None, :]
    )
    live_rows = slot_adapter_index < ADAPTER_COUNT
    new_state = jnp.where(live_rows[:, None, None, None], fresh, old_state).reshape(state.shape)
    read_out = (
        jnp.sum(fresh * output_mat[:, None, None, :], axis=3)
        + head_skip_gain[None, :, None] * x_heads
    )
    gated = read_out.reshape(own_rows, inner) * jax.nn.silu(z_part)
    gate_squares = jnp.sum(gated * gated, axis=1, keepdims=True)
    mixed = jnp.where(
        live_rows[:, None], gated * gate_norm_gain.astype(f32)[None, :], 0.0
    ).astype(bf16)
    gate_high, gate_low = halves(gate_squares)
    mixed_all = spread_all(
        jnp.concatenate([mixed, fill([gate_high, gate_low])], axis=1), "dp", dp_count
    ).reshape(all_rows, inner + LANES)

    output_table = jnp.transpose(adapter_output_down, (1, 0, 2)).reshape(inner, lane_groups)
    joined_out = jnp.concatenate([mixer_output_weight, output_table], axis=1)
    mixed_main = jnp.dot(mixed_all[:, :inner], joined_out, preferred_element_type=f32)
    low_out = jnp.where(lane_pick, mixed_main[:, local_width:], 0.0)
    terms = mixed_main[:, :local_width] + split_dot(
        low_out, adapter_output_up.reshape(lane_groups, local_width)
    )
    mixer_sent = jnp.concatenate([terms.astype(bf16), mixed_all[:, inner:]], axis=1)
    quad = 4
    quad_groups = [list(range(q, q + quad)) for q in range(0, head_count, quad)]
    quad_rows = all_rows // quad
    parts = trade(
        mixer_sent.reshape(quad, quad_rows, mixer_sent.shape[1]), "head", quad_groups
    ).astype(f32)
    part_squares = parts[:, :, local_width : local_width + 1] + parts[
        :, :, local_width + 1 : local_width + 2
    ]
    group_squares = jnp.sum(
        part_squares.reshape(quad // shares, shares, quad_rows, 1), axis=1, keepdims=True
    )
    group_scale = lax.rsqrt(group_squares / (HEAD_TOTAL * HEAD_CHANNELS // GROUPS) + eps)
    quad_sum = jnp.sum(
        parts[:, :, :local_width].reshape(quad // shares, shares, quad_rows, local_width)
        * group_scale,
        axis=(0, 1),
    ).astype(bf16)
    mixer_all = jnp.sum(
        spread_all(quad_sum, "head", head_count)
        .astype(f32)
        .reshape(head_count // quad, quad * quad_rows, local_width),
        axis=0,
    )
    resid_all = (wide + mixer_all).astype(bf16)
    resid_wide = resid_all.astype(f32)
    mlp_squares = jnp.sum(resid_wide * resid_wide, axis=1, keepdims=True)
    mlp_in = (resid_wide * mlp_norm_gain.astype(f32)[None, :]).astype(bf16)
    resid_rows = lax.dynamic_slice_in_dim(resid_all, head_index * rows_head, rows_head, 0)
    up = jnp.dot(mlp_in, mlp_up_weight, preferred_element_type=f32).astype(bf16)
    mlp_high, mlp_low = halves(mlp_squares)
    up_sent = jnp.concatenate([up, fill([mlp_high, mlp_low])], axis=1)
    up_sum = jnp.sum(
        trade(up_sent.reshape(dp_count, own_rows, up_sent.shape[1]), "dp").astype(f32), axis=0
    )
    row_squares = (
        up_sum[:, hidden_here : hidden_here + 1] + up_sum[:, hidden_here + 1 : hidden_here + 2]
    )
    mlp_scale = lax.rsqrt(row_squares / MODEL_WIDTH + eps)
    hidden = (jnp.maximum(up_sum[:, :hidden_here] * mlp_scale, 0.0) ** 2).astype(bf16)
    hidden_all = spread_all(hidden, "dp", dp_count).reshape(all_rows, hidden_here)
    down = jnp.dot(hidden_all, mlp_down_weight, preferred_element_type=f32).astype(bf16)
    down_rows = jnp.sum(
        trade(down.reshape(head_count, rows_head, local_width), "head").astype(f32), axis=0
    )
    out_stream = (resid_rows.astype(f32) + down_rows).astype(bf16)
    return (out_stream, new_state)


def solution(mesh):
    in_specs = (
        P("head", "dp"),
        P("dp", "head", None),
        P("dp"),
        P("dp", "head"),
        P("dp", "head"),
        P("dp", "head"),
        P("dp", "head"),
        P("head"),
        P("head"),
        P("head"),
        P("head"),
        P("head", "dp"),
        P(None, "dp", None),
        P(None, None, None, "head"),
        P(None, "head", None),
        P(None, None, "dp"),
        P("dp"),
        P("dp", "head"),
        P("head", "dp"),
        P("dp"),
        P(),
    )
    out_specs = (P("head", "dp"), P("dp", "head", None))
    return jax.shard_map(
        per_device, mesh=mesh, in_specs=in_specs, out_specs=out_specs, check_vma=False
    )
```

time: 1050 us -> 155 us (0.15)
  the two profiles are of different devices: /device:TPU:16 before, /device:TPU:2 now
where the time goes in v1:
time: 155 us; the launch traced here: 154 us
  waiting for transfers between devices  61.5 us (40%)
  starting transfers between devices  47.1 us (30%)
  blocking collectives  24.8 us (16%)
  local copies, waits for them, and re-layouts  12.1 us (8%)
  other arithmetic  4.89 us (3%)
  matrix products  2.05 us (1%)
    all_to_all x4, waiting for transfers between devices, spread_all(): return lax.all_to_all(copies, axis, 0, 0)  40 us
    all_to_all x2, blocking collectives, trade(): return lax.all_to_all(blocks, axis, 0, 0, axis_index_groups=groups)  24.8 us
    all_to_all x4, starting transfers between devices, spread_all(): return lax.all_to_all(copies, axis, 0, 0)  23.9 us
    all_to_all x2, waiting for transfers between devices, trade(): return lax.all_to_all(blocks, axis, 0, 0, axis_index_groups=groups)  21.5 us
    all_to_all x2, starting transfers between devices, trade(): return lax.all_to_all(blocks, axis, 0, 0, axis_index_groups=groups)  16.2 us
    unnamed x43, local copies, waits for them, and re-layouts  6.19 us
    ppermute x1, starting transfers between devices, per_device(): second_map = lax.ppermute(group_map_weight, 'head', second_move)  5.48 us
    broadcast_in_dim x4, local copies, waits for them, and re-layouts, spread_all(): copies = jnp.broadcast_to(block[None], (count,) + block.shape)  3.55 us
  transfers between devices with their start and end apart: 8, of which 6 were waited for; matrix products, arithmetic and copies ran while one was open for 3% of the time, Pallas kernels for 0%

profile of v1, /device:TPU:2, one launch (start us, length us, event | category | flops | bytes accessed | tf_op | source)
XLA Modules:
  0.0 153.6 jit_solution(10164684290410400311)
XLA Ops:
  0.6 1.6 %collective-permute-start = (bf16[256,128]{1,0:T(8,128)(2,1)}, bf16[256,128]{1,0:T(8,128)(2,1)S(1)}, u32[]{:S(2)}, u32[]{:S(2)}) collective-permute-start(bf16[256,128]{1,0:T(8,128)(2,1)} %param.26), channel_id=1, source_target_pairs={{0,0},{8,1},{1,2},{9,3},{2,4},{10,5},{3,6},{11,7},{4,8},{12,9},{5,... | collective-permute-start | bytes 196616 | tf_op jit(solution)/shard_map/ppermute | solution.py:88
  2.3 5.5 %collective-permute-start.1 = (bf16[256,128]{1,0:T(8,128)(2,1)}, bf16[256,128]{1,0:T(8,128)(2,1)S(1)}, u32[]{:S(2)}, u32[]{:S(2)}) collective-permute-start(bf16[256,128]{1,0:T(8,128)(2,1)} %param.26), channel_id=1, source_target_pairs={{8,0},{0,1},{9,2},{1,3},{10,4},{2,5},{11,6},{3,7},{12,8},{4,9},{13... | collective-permute-start | bytes 196616 | tf_op jit(solution)/shard_map/ppermute | solution.py:89
  7.8 1.3 broadcast_in_dim.29
  9.1 10.9 %all-to-all-start = ((bf16[16,8,256]{2,1,0:T(8,128)(2,1)}), bf16[16,8,256]{2,1,0:T(8,128)(2,1)S(1)}, u32[]{:S(2)}, u32[]{:S(2)}) async-start(bf16[16,8,256]{2,1,0:T(8,128)(2,1)} %broadcast_in_dim.29), calls=%async_computation | async-start | bytes 131072 | tf_op jit(solution)/shard_map/all_to_all | solution.py:40
  20.1 0.6 copy-done.14
  20.7 1.0 constant_dynamic-update-slice_fusion.4
  22.6 7.5 %all-to-all-done = bf16[16,8,256]{2,1,0:T(8,128)(2,1)S(1)} async-done(((bf16[16,8,256]{2,1,0:T(8,128)(2,1)}), bf16[16,8,256]{2,1,0:T(8,128)(2,1)S(1)}, u32[]{:S(2)}, u32[]{:S(2)}) %all-to-all-start) | async-done | bytes 65568 | tf_op jit(solution)/shard_map/all_to_all | solution.py:40
  30.3 0.6 copy-done.13
  31.6 0.8 reshape.225
  32.4 12.1 %all-to-all-start.1 = ((bf16[32,4,1536]{2,1,0:T(4,128)(2,1)}), bf16[32,4,1536]{2,1,0:T(4,128)(2,1)S(1)}, u32[]{:S(2)}, u32[]{:S(2)}) async-start(bf16[32,4,1536]{2,1,0:T(4,128)(2,1)} %reshape.225), calls=%async_computation.1 | async-start | bytes 786432 | tf_op jit(solution)/shard_map/all_to_all | solution.py:44
  44.6 0.6 copy-done.9
  45.3 0.6 copy-done.8
  46.0 0.7 copy-done.16
  46.6 12.8 %all-to-all-done.1 = bf16[32,4,1536]{2,1,0:T(4,128)(2,1)S(1)} async-done(((bf16[32,4,1536]{2,1,0:T(4,128)(2,1)}), bf16[32,4,1536]{2,1,0:T(4,128)(2,1)S(1)}, u32[]{:S(2)}, u32[]{:S(2)}) %all-to-all-start.1) | async-done | bytes 393248 | tf_op jit(solution)/shard_map/all_to_all | solution.py:44
  61.0 0.7 fusion.5
  62.2 0.7 broadcast_in_dim.33
  63.0 4.2 %all-to-all-start.2 = ((bf16[32,4,640]{2,1,0:T(4,128)(2,1)}), bf16[32,4,640]{2,1,0:T(4,128)(2,1)S(1)}, u32[]{:S(2)}, u32[]{:S(2)}) async-start(bf16[32,4,640]{2,1,0:T(4,128)(2,1)} %broadcast_in_dim.33), calls=%async_computation.2 | async-start | bytes 327680 | tf_op jit(solution)/shard_map/all_to_all | solution.py:40
  67.3 9.9 %all-to-all-done.2 = bf16[32,4,640]{2,1,0:T(4,128)(2,1)S(1)} async-done(((bf16[32,4,640]{2,1,0:T(4,128)(2,1)}), bf16[32,4,640]{2,1,0:T(4,128)(2,1)S(1)}, u32[]{:S(2)}, u32[]{:S(2)}) %all-to-all-start.2) | async-done | bytes 163872 | tf_op jit(solution)/shard_map/all_to_all | solution.py:40
  77.6 0.7 copy-done.7
  78.6 8.2 %all_to_all.40 = bf16[4,32,384]{2,1,0:T(8,128)(2,1)S(1)} all-to-all(bf16[4,32,384]{2,1,0:T(8,128)(2,1)S(1)} %bitcast.67), channel_id=1, replica_groups={{0,1,2,3},{4,5,6,7},{8,9,10,11},{12,13,14,15},{16,17,18,19},{20,21,22,2..., dimensions={0} | all-to-all | bytes 196608 | tf_op jit(solution)/shard_map/all_to_all | solution.py:44
  87.1 0.7 broadcast_in_dim.38
  87.9 4.6 %all-to-all-start.4 = ((bf16[16,32,256]{2,1,0:T(8,128)(2,1)}), bf16[16,32,256]{2,1,0:T(8,128)(2,1)S(1)}, u32[]{:S(2)}, u32[]{:S(2)}) async-start(bf16[16,32,256]{2,1,0:T(8,128)(2,1)} %broadcast_in_dim.38), calls=%async_computation.4 | async-start | bytes 524288 | tf_op jit(solution)/shard_map/all_to_all | solution.py:40
  92.5 10.6 %all-to-all-done.4 = bf16[16,32,256]{2,1,0:T(8,128)(2,1)S(1)} async-done(((bf16[16,32,256]{2,1,0:T(8,128)(2,1)}), bf16[16,32,256]{2,1,0:T(8,128)(2,1)S(1)}, u32[]{:S(2)}, u32[]{:S(2)}) %all-to-all-start.4) | async-done | bytes 262176 | tf_op jit(solution)/shard_map/all_to_all | solution.py:40
  103.9 16.6 %all_to_all.41 = bf16[32,4,1152]{2,1,0:T(4,128)(2,1)S(1)} all-to-all(bf16[32,4,1152]{2,1,0:T(4,128)(2,1)S(1)} %reshape.236), channel_id=1, replica_groups=mesh['dp'=32,'head'=16] {'dp'}, dimensions={0} | all-to-all | bytes 589824 | tf_op jit(solution)/shard_map/all_to_all | solution.py:44
  120.9 0.8 broadcast_in_dim.39
  121.6 4.1 %all-to-all-start.6 = ((bf16[32,4,1024]{2,1,0:T(4,128)(2,1)}), bf16[32,4,1024]{2,1,0:T(4,128)(2,1)S(1)}, u32[]{:S(2)}, u32[]{:S(2)}) async-start(bf16[32,4,1024]{2,1,0:T(4,128)(2,1)} %broadcast_in_dim.39), calls=%async_computation.6 | async-start | bytes 524288 | tf_op jit(solution)/shard_map/all_to_all | solution.py:40
  125.9 12.0 %all-to-all-done.6 = bf16[32,4,1024]{2,1,0:T(4,128)(2,1)S(1)} async-done(((bf16[32,4,1024]{2,1,0:T(4,128)(2,1)}), bf16[32,4,1024]{2,1,0:T(4,128)(2,1)S(1)}, u32[]{:S(2)}, u32[]{:S(2)}) %all-to-all-start.6) | async-done | bytes 262176 | tf_op jit(solution)/shard_map/all_to_all | solution.py:40
  138.0 0.9 fusion
  138.8 4.1 %all-to-all-start.7 = ((bf16[16,8,256]{2,1,0:T(8,128)(2,1)}), bf16[16,8,256]{2,1,0:T(8,128)(2,1)S(1)}, u32[]{:S(2)}, u32[]{:S(2)}) async-start(bf16[16,8,256]{2,1,0:T(8,128)(2,1)} %fusion), calls=%async_computation.7 | async-start | bytes 131072 | tf_op jit(solution)/shard_map/all_to_all | solution.py:44
  142.9 1.3 fusion.2
  144.3 8.7 %all-to-all-done.7 = bf16[16,8,256]{2,1,0:T(8,128)(2,1)S(1)} async-done(((bf16[16,8,256]{2,1,0:T(8,128)(2,1)}), bf16[16,8,256]{2,1,0:T(8,128)(2,1)S(1)}, u32[]{:S(2)}, u32[]{:S(2)}) %all-to-all-start.7) | async-done | bytes 65568 | tf_op jit(solution)/shard_map/all_to_all | solution.py:44
  153.0 0.6 add_convert_fusion
  (107 shorter events, 6.3 us)
Async XLA Ops:
  0.6 102.9 %copy-start = (bf16[256,1024]{1,0:T(8,128)(2,1)S(1)}, bf16[256,1024]{1,0:T(8,128)(2,1)}, u32[]{:S(2)}) copy-start(bf16[256,1024]{1,0:T(8,128)(2,1)} %param.38) | copy-start | bytes 1572868
  0.6 21.9 %collective-permute-start = (bf16[256,128]{1,0:T(8,128)(2,1)}, bf16[256,128]{1,0:T(8,128)(2,1)S(1)}, u32[]{:S(2)}, u32[]{:S(2)}) collective-permute-start(bf16[256,128]{1,0:T(8,128)(2,1)} %param.26), channel_id=1, source_target_pairs={{0,0},{8,1},{1,2},{9,3},{2,4},{10,5},{3,6},{11,7},{4,8},{12,9},{5,... | collective-permute-start | bytes 196616 | tf_op jit(solution)/shard_map/ppermute | solution.py:88
  2.3 20.3 %collective-permute-start.1 = (bf16[256,128]{1,0:T(8,128)(2,1)}, bf16[256,128]{1,0:T(8,128)(2,1)S(1)}, u32[]{:S(2)}, u32[]{:S(2)}) collective-permute-start(bf16[256,128]{1,0:T(8,128)(2,1)} %param.26), channel_id=1, source_target_pairs={{8,0},{0,1},{9,2},{1,3},{10,4},{2,5},{11,6},{3,7},{12,8},{4,9},{13... | collective-permute-start | bytes 196616 | tf_op jit(solution)/shard_map/ppermute | solution.py:89
  9.1 21.0 %all-to-all-start = ((bf16[16,8,256]{2,1,0:T(8,128)(2,1)}), bf16[16,8,256]{2,1,0:T(8,128)(2,1)S(1)}, u32[]{:S(2)}, u32[]{:S(2)}) async-start(bf16[16,8,256]{2,1,0:T(8,128)(2,1)} %broadcast_in_dim.29), calls=%async_computation | async-start | bytes 131072 | tf_op jit(solution)/shard_map/all_to_all | solution.py:40
  20.0 0.7 copy-start.14
  20.7 1.0 copy-start.6
  20.7 1.8 %copy-start.3 = (bf16[256,512]{1,0:T(8,128)(2,1)S(1)}, bf16[256,512]{1,0:T(8,128)(2,1)}, u32[]{:S(2)}) copy-start(bf16[256,512]{1,0:T(8,128)(2,1)} %param.25) | copy-start | bytes 786436
  21.7 0.7 copy-start.15
  30.2 0.7 copy-start.13
  31.6 12.9 %copy-start.4 = (bf16[8,16,2,512]{3,2,1,0:T(2,128)(2,1)S(1)}, bf16[8,16,2,512]{3,2,1,0:T(2,128)(2,1)}, u32[]{:S(2)}) copy-start(bf16[8,16,2,512]{3,2,1,0:T(2,128)(2,1)} %param.34) | copy-start | bytes 786436
  32.4 28.6 %copy-start.1 = (f32[4,8,8192]{2,1,0:T(8,128)S(1)}, f32[4,8,8192]{2,1,0:T(8,128)}, u32[]{:S(2)}) copy-start(f32[4,8,8192]{2,1,0:T(8,128)} %param.22) | copy-start | bytes 3145732
  32.4 27.0 %all-to-all-start.1 = ((bf16[32,4,1536]{2,1,0:T(4,128)(2,1)}), bf16[32,4,1536]{2,1,0:T(4,128)(2,1)S(1)}, u32[]{:S(2)}, u32[]{:S(2)}) async-start(bf16[32,4,1536]{2,1,0:T(4,128)(2,1)} %reshape.225), calls=%async_computation.1 | async-start | bytes 786432 | tf_op jit(solution)/shard_map/all_to_all | solution.py:44
  44.5 0.7 copy-start.9
  45.3 0.7 copy-start.8
  45.9 0.7 copy-start.16
  60.1 0.7 copy-start.10
  60.1 0.7 copy-start.11
  63.0 4.2 %copy-start.5 = (bf16[8,512,16]{1,2,0:T(8,128)(2,1)S(1)}, bf16[8,512,16]{1,2,0:T(8,128)(2,1)}, u32[]{:S(2)}) copy-start(bf16[8,512,16]{1,2,0:T(8,128)(2,1)} %param.35) | copy-start | bytes 393220
  63.0 14.3 %all-to-all-start.2 = ((bf16[32,4,640]{2,1,0:T(4,128)(2,1)}), bf16[32,4,640]{2,1,0:T(4,128)(2,1)S(1)}, u32[]{:S(2)}, u32[]{:S(2)}) async-start(bf16[32,4,640]{2,1,0:T(4,128)(2,1)} %broadcast_in_dim.33), calls=%async_computation.2 | async-start | bytes 327680 | tf_op jit(solution)/shard_map/all_to_all | solution.py:40
  67.3 10.0 %copy-start.12 = (bf16[512,256]{1,0:T(8,128)(2,1)S(1)}, bf16[512,256]{1,0:T(8,128)(2,1)}, u32[]{:S(2)}) copy-start(bf16[512,256]{1,0:T(8,128)(2,1)} %param.32) | copy-start | bytes 786436
  77.5 0.8 copy-start.7
  87.9 4.6 %copy-start.17 = (bf16[256]{0:T(256)(128)(2,1)S(1)}, bf16[256]{0:T(256)(128)(2,1)}, u32[]{:S(2)}) copy-start(bf16[256]{0:T(256)(128)(2,1)} %param.37) | copy-start | bytes 1540
  87.9 15.2 %all-to-all-start.4 = ((bf16[16,32,256]{2,1,0:T(8,128)(2,1)}), bf16[16,32,256]{2,1,0:T(8,128)(2,1)S(1)}, u32[]{:S(2)}, u32[]{:S(2)}) async-start(bf16[16,32,256]{2,1,0:T(8,128)(2,1)} %broadcast_in_dim.38), calls=%async_computation.4 | async-start | bytes 524288 | tf_op jit(solution)/shard_map/all_to_all | solution.py:40
  121.6 16.3 %all-to-all-start.6 = ((bf16[32,4,1024]{2,1,0:T(4,128)(2,1)}), bf16[32,4,1024]{2,1,0:T(4,128)(2,1)S(1)}, u32[]{:S(2)}, u32[]{:S(2)}) async-start(bf16[32,4,1024]{2,1,0:T(4,128)(2,1)} %broadcast_in_dim.39), calls=%async_computation.6 | async-start | bytes 524288 | tf_op jit(solution)/shard_map/all_to_all | solution.py:40
  125.7 12.2 %copy-start.2 = (bf16[1024,256]{1,0:T(8,128)(2,1)S(1)}, bf16[1024,256]{1,0:T(8,128)(2,1)}, u32[]{:S(2)}) copy-start(bf16[1024,256]{1,0:T(8,128)(2,1)} %param.39) | copy-start | bytes 1572868
  138.8 14.1 %all-to-all-start.7 = ((bf16[16,8,256]{2,1,0:T(8,128)(2,1)}), bf16[16,8,256]{2,1,0:T(8,128)(2,1)S(1)}, u32[]{:S(2)}, u32[]{:S(2)}) async-start(bf16[16,8,256]{2,1,0:T(8,128)(2,1)} %fusion), calls=%async_computation.7 | async-start | bytes 131072 | tf_op jit(solution)/shard_map/all_to_all | solution.py:44

commit v2 on v1

--- a/solution.py
+++ b/solution.py
@@ -28,11 +28,6 @@
     rows = value.shape[0]
     both = jnp.dot(jnp.concatenate([high, low], axis=0), weight, preferred_element_type=f32)
     return both[:rows] + both[rows:]
-
-
-def fill(columns):
-    joined = jnp.concatenate(columns, axis=1)
-    return jnp.pad(joined, ((0, 0), (0, -joined.shape[1] % LANES)))
 
 
 def spread_all(block, axis, count):
@@ -88,85 +83,156 @@
     first_map = lax.ppermute(group_map_weight, "head", first_move)
     second_map = lax.ppermute(group_map_weight, "head", second_move)
 
-    gathered = spread_all(stream, "head", head_count).reshape(all_rows, local_width)
-    wide = gathered.astype(f32)
-    gained = (wide * mixer_norm_gain.astype(f32)[None, :]).astype(bf16)
-    mix_squares = jnp.sum(wide * wide, axis=1, keepdims=True)
-
     row_tile = jnp.arange(all_rows, dtype=jnp.int32) // TILE * TILE
     row_adapter = (
         jnp.sum((segment_first_slot[None, :] <= row_tile[:, None]).astype(jnp.int32), axis=1) - 1
     )
+    lane = jnp.arange(LANES, dtype=jnp.int32)
     lane_adapter = jnp.arange(lane_groups, dtype=jnp.int32) // ADAPTER_RANK
-    lane_pick = row_adapter[:, None] == lane_adapter[None, :]
+    lane_pick = (row_adapter[:, None] == lane_adapter[None, :]).astype(bf16)
+    own_pick = lax.dynamic_slice_in_dim(lane_pick, dp_index * own_rows, own_rows, 0).astype(f32)
     input_table = jnp.transpose(adapter_input_down, (1, 0, 2)).reshape(local_width, lane_groups)
     joined = jnp.concatenate(
-        [head_input_weight, output_gate_weight, first_map, second_map, input_table], axis=1
-    )
-    main = jnp.dot(gained, joined, preferred_element_type=f32)
-    map_end = 2 * inner + 2 * NSTATE
-    low = jnp.where(lane_pick, main[:, map_end:], 0.0).astype(bf16)
-    step = jnp.dot(gained, step_size_weight, preferred_element_type=f32)
-    step_high, step_low = halves(step)
-    squares_high, squares_low = halves(mix_squares)
-    sent = jnp.concatenate(
-        [main[:, :map_end].astype(bf16), low, fill([step_high, step_low, squares_high, squares_low])],
+        [head_input_weight, output_gate_weight, first_map, second_map], axis=1
+    )
+    joined_tail = jnp.concatenate(
+        [
+            input_table,
+            step_size_weight,
+            step_size_weight,
+            jnp.zeros((local_width, LANES - 2 * heads_here), bf16),
+        ],
         axis=1,
     )
+    at_squares = 2 * heads_here
+    at_rank = at_squares + 8
+    rank_here = jnp.arange(lane_groups, dtype=jnp.int32)[:, None] % ADAPTER_RANK
+    fold = (rank_here + at_rank == lane[None, :]).astype(bf16)
+    up_table = adapter_input_up.reshape(lane_groups, 2 * inner)
+    output_table = jnp.transpose(adapter_output_down, (1, 0, 2)).reshape(inner, lane_groups)
+    joined_out = jnp.concatenate([mixer_output_weight, output_table], axis=1)
+    output_lift = adapter_output_up.reshape(lane_groups, local_width)
+    live = jnp.broadcast_to(
+        (slot_adapter_index < ADAPTER_COUNT).astype(f32)[:, None], (own_rows, LANES)
+    )
+    mixer_gain = mixer_norm_gain.astype(f32)[None, :]
+    mlp_gain = mlp_norm_gain.astype(f32)[None, :]
+    gate_gain = gate_norm_gain.astype(f32)[None, :]
+    skip_gain = jnp.repeat(head_skip_gain, HEAD_CHANNELS)[None, :]
+    input_first = jnp.broadcast_to((head_index % shares == 0).astype(f32), (1, LANES))
+    input_second = 1.0 - input_first
+    head_row = (head_index * rows_head).astype(jnp.uint32)
+    pick_first = (lane[None, :] == 0).astype(f32)
+    pick_second = (lane[None, :] == 1).astype(f32)
+    live_inner = jnp.broadcast_to(live[:, :1], (own_rows, inner)) * gate_gain
+    gathered = spread_all(stream, "head", head_count)
+    (
+        gathered,
+        lane_pick,
+        own_pick,
+        joined,
+        joined_tail,
+        fold,
+        up_table,
+        joined_out,
+        output_lift,
+        live,
+        mixer_gain,
+        mlp_gain,
+        skip_gain,
+        input_first,
+        input_second,
+        head_row,
+        pick_first,
+        pick_second,
+        live_inner,
+        step_size_bias,
+        head_decay_rate,
+        stream,
+    ) = lax.optimization_barrier(
+        (
+            gathered,
+            lane_pick,
+            own_pick,
+            joined,
+            joined_tail,
+            fold,
+            up_table,
+            joined_out,
+            output_lift,
+            live,
+            mixer_gain,
+            mlp_gain,
+            skip_gain,
+            input_first,
+            input_second,
+            head_row,
+            pick_first,
+            pick_second,
+            live_inner,
+            step_size_bias,
+            head_decay_rate,
+            stream,
+        )
+    )
+    wide = gathered.reshape(all_rows, local_width).astype(f32)
+    gained = (wide * mixer_gain).astype(bf16)
+    mix_squares = jnp.sum(wide * wide, axis=1, keepdims=True)
+    main = jnp.dot(gained, joined, preferred_element_type=f32).astype(bf16)
+    tail = jnp.dot(gained, joined_tail, preferred_element_type=f32)
+    low = jnp.dot(tail[:, :lane_groups].astype(bf16) * lane_pick, fold, preferred_element_type=f32)
+    step = tail[:, lane_groups:]
+    column = lane[None, :]
+    wanted = jnp.where(column < at_squares, step, mix_squares)
+    high = lax.reduce_precision(wanted, exponent_bits=8, mantissa_bits=7)
+    is_high = (column < heads_here) | (column == at_squares)
+    exact = jnp.where(is_high, high, wanted - high)
+    last = jnp.where(column < at_rank, exact, low).astype(bf16)
+    sent = jnp.concatenate([main, last], axis=1)
     summed = jnp.sum(
         trade(sent.reshape(dp_count, own_rows, sent.shape[1]), "dp").astype(f32), axis=0
     )
-    tail = map_end + lane_groups
-    squares = summed[:, tail + 2 * heads_here : tail + 2 * heads_here + 1] + summed[
-        :, tail + 2 * heads_here + 1 : tail + 2 * heads_here + 2
-    ]
+    map_end = 2 * inner + 2 * NSTATE
+    last = summed[:, map_end:]
+    squares = last[:, at_squares : at_squares + 1] + last[:, at_squares + 1 : at_squares + 2]
     mix_scale = lax.rsqrt(squares / MODEL_WIDTH + eps)
     projected = summed * mix_scale
-    low_rank = projected[:, map_end:tail]
-    lift = split_dot(low_rank, adapter_input_up.reshape(lane_groups, 2 * inner))
+    last = last * mix_scale
+    low_rank = last[:, at_rank : at_rank + ADAPTER_RANK]
+    spread_low = jnp.concatenate([low_rank] * ADAPTER_COUNT, axis=1) * own_pick
+    lift = split_dot(spread_low, up_table)
     x_part = projected[:, :inner] + lift[:, :inner]
     z_part = projected[:, inner : 2 * inner] + lift[:, inner:]
-    step_raw = (
-        projected[:, tail : tail + heads_here]
-        + projected[:, tail + heads_here : tail + 2 * heads_here]
-    )
+    step_raw = last[:, :heads_here] + last[:, heads_here : 2 * heads_here]
     first_part = projected[:, 2 * inner : 2 * inner + NSTATE]
     second_part = projected[:, 2 * inner + NSTATE : map_end]
-    input_first = head_index % shares == 0
-    input_mat = jax.nn.silu(jnp.where(input_first, first_part, second_part))
-    output_mat = jax.nn.silu(jnp.where(input_first, second_part, first_part))
+    input_mat = jax.nn.silu(first_part * input_first + second_part * input_second)
+    output_mat = jax.nn.silu(second_part * input_first + first_part * input_second)
 
     step_size = jax.nn.softplus(step_raw + step_size_bias[None, :])
     forget = jnp.exp(-step_size * head_decay_rate[None, :])
     x_heads = jax.nn.silu(x_part).reshape(own_rows, heads_here, HEAD_CHANNELS)
     old_state = state.reshape(own_rows, heads_here, HEAD_CHANNELS, NSTATE)
+    step_x = step_size[:, :, None] * x_heads
     fresh = (
-        forget[:, :, None, None] * old_state
-        + (step_size[:, :, None] * x_heads)[:, :, :, None] * input_mat[:, None, None, :]
-    )
-    live_rows = slot_adapter_index < ADAPTER_COUNT
-    new_state = jnp.where(live_rows[:, None, None, None], fresh, old_state).reshape(state.shape)
+        forget[:, :, None, None] * old_state + step_x[:, :, :, None] * input_mat[:, None, None, :]
+    )
     read_out = (
-        jnp.sum(fresh * output_mat[:, None, None, :], axis=3)
-        + head_skip_gain[None, :, None] * x_heads
-    )
-    gated = read_out.reshape(own_rows, inner) * jax.nn.silu(z_part)
+        jnp.sum(fresh * output_mat[:, None, None, :], axis=3).reshape(own_rows, inner)
+        + skip_gain * x_heads.reshape(own_rows, inner)
+    )
+    gated = read_out * jax.nn.silu(z_part)
     gate_squares = jnp.sum(gated * gated, axis=1, keepdims=True)
-    mixed = jnp.where(
-        live_rows[:, None], gated * gate_norm_gain.astype(f32)[None, :], 0.0
-    ).astype(bf16)
-    gate_high, gate_low = halves(gate_squares)
+    mixed = (gated * live_inner).astype(bf16)
+    gate_high = lax.reduce_precision(gate_squares, exponent_bits=8, mantissa_bits=7)
+    gate_tail = (gate_high * pick_first + (gate_squares - gate_high) * pick_second).astype(bf16)
     mixed_all = spread_all(
-        jnp.concatenate([mixed, fill([gate_high, gate_low])], axis=1), "dp", dp_count
+        jnp.concatenate([mixed, gate_tail], axis=1), "dp", dp_count
     ).reshape(all_rows, inner + LANES)
 
-    output_table = jnp.transpose(adapter_output_down, (1, 0, 2)).reshape(inner, lane_groups)
-    joined_out = jnp.concatenate([mixer_output_weight, output_table], axis=1)
     mixed_main = jnp.dot(mixed_all[:, :inner], joined_out, preferred_element_type=f32)
-    low_out = jnp.where(lane_pick, mixed_main[:, local_width:], 0.0)
-    terms = mixed_main[:, :local_width] + split_dot(
-        low_out, adapter_output_up.reshape(lane_groups, local_width)
-    )
+    low_out = mixed_main[:, local_width:] * lane_pick.astype(f32)
+    terms = mixed_main[:, :local_width] + split_dot(low_out, output_lift)
     mixer_sent = jnp.concatenate([terms.astype(bf16), mixed_all[:, inner:]], axis=1)
     quad = 4
     quad_groups = [list(range(q, q + quad)) for q in range(0, head_count, quad)]
@@ -195,11 +261,13 @@
     resid_all = (wide + mixer_all).astype(bf16)
     resid_wide = resid_all.astype(f32)
     mlp_squares = jnp.sum(resid_wide * resid_wide, axis=1, keepdims=True)
-    mlp_in = (resid_wide * mlp_norm_gain.astype(f32)[None, :]).astype(bf16)
-    resid_rows = lax.dynamic_slice_in_dim(resid_all, head_index * rows_head, rows_head, 0)
+    mlp_in = (resid_wide * mlp_gain).astype(bf16)
     up = jnp.dot(mlp_in, mlp_up_weight, preferred_element_type=f32).astype(bf16)
-    mlp_high, mlp_low = halves(mlp_squares)
-    up_sent = jnp.concatenate([up, fill([mlp_high, mlp_low])], axis=1)
+    mlp_high = lax.reduce_precision(mlp_squares, exponent_bits=8, mantissa_bits=7)
+    up_tail = (mlp_high * pick_first + (mlp_squares - mlp_high) * pick_second).astype(bf16)
+    up_sent = jnp.concatenate([up, up_tail], axis=1)
+    resid_rows = lax.dynamic_slice_in_dim(resid_all, head_row, rows_head, 0)
+    up_sent, resid_rows = lax.optimization_barrier((up_sent, resid_rows))
     up_sum = jnp.sum(
         trade(up_sent.reshape(dp_count, own_rows, up_sent.shape[1]), "dp").astype(f32), axis=0
     )
@@ -210,6 +278,13 @@
     hidden = (jnp.maximum(up_sum[:, :hidden_here] * mlp_scale, 0.0) ** 2).astype(bf16)
     hidden_all = spread_all(hidden, "dp", dp_count).reshape(all_rows, hidden_here)
     down = jnp.dot(hidden_all, mlp_down_weight, preferred_element_type=f32).astype(bf16)
+    down, old_state, live, forget, step_x, input_mat = lax.optimization_barrier(
+        (down, old_state, live, forget, step_x, input_mat)
+    )
+    fresh = (
+        forget[:, :, None, None] * old_state + step_x[:, :, :, None] * input_mat[:, None, None, :]
+    )
+    new_state = jnp.where(live[:, 0, None, None, None] > 0, fresh, old_state).reshape(state.shape)
     down_rows = jnp.sum(
         trade(down.reshape(head_count, rows_head, local_width), "head").astype(f32), axis=0
     )

time: 155 us -> 146 us (0.942)
  blocking collectives: 24.8 us -> 94.5 us
  waiting for transfers between devices: 61.5 us -> 14.9 us
  starting transfers between devices: 47.1 us -> 21.9 us
  local copies, waits for them, and re-layouts: 12.1 us -> 4.85 us
    all_to_all x0 -> x3, blocking collectives: none -> 43.5 us  [spread_all(): return lax.all_to_all(copies, axis, 0, 0)]
    all_to_all x4 -> x1, waiting for transfers between devices: 40 us -> 6.34 us  [spread_all(): return lax.all_to_all(copies, axis, 0, 0)]
    all_to_all x2 -> x3, blocking collectives: 24.8 us -> 51 us  [trade(): return lax.all_to_all(blocks, axis, 0, 0, axis_index_groups=groups)]
    all_to_all x2 -> x1, waiting for transfers between devices: 21.5 us -> 8.59 us  [trade(): return lax.all_to_all(blocks, axis, 0, 0, axis_index_groups=groups)]
    all_to_all x2 -> x1, starting transfers between devices: 16.2 us -> 4.06 us  [trade(): return lax.all_to_all(blocks, axis, 0, 0, axis_index_groups=groups)]
    all_to_all x4 -> x1, starting transfers between devices: 23.9 us -> 12.7 us  [spread_all(): return lax.all_to_all(copies, axis, 0, 0)]
    unnamed x43 -> x33, local copies, waits for them, and re-layouts: 6.19 us -> 1.06 us
    broadcast_in_dim x4, local copies, waits for them, and re-layouts: 3.55 us -> 1.46 us  [spread_all(): copies = jnp.broadcast_to(block[None], (count,) + block.shape)]
  transfers between devices with their start and end apart: 8 -> 4, of which waited for: 6 -> 2; matrix products, arithmetic and copies ran while one was open for 3% -> 4% of each run, Pallas kernels for 0% -> 0%
where the time goes in v2:
time: 146 us
  blocking collectives  94.5 us (65%)
  starting transfers between devices  21.9 us (15%)
  waiting for transfers between devices  14.9 us (10%)
  other arithmetic  5.95 us (4%)
  local copies, waits for them, and re-layouts  4.85 us (3%)
  matrix products  2.22 us (2%)
    all_to_all x3, blocking collectives, trade(): return lax.all_to_all(blocks, axis, 0, 0, axis_index_groups=groups)  51 us
    all_to_all x3, blocking collectives, spread_all(): return lax.all_to_all(copies, axis, 0, 0)  43.5 us
    all_to_all x1, starting transfers between devices, spread_all(): return lax.all_to_all(copies, axis, 0, 0)  12.7 us
    all_to_all x1, waiting for transfers between devices, trade(): return lax.all_to_all(blocks, axis, 0, 0, axis_index_groups=groups)  8.59 us
    all_to_all x1, waiting for transfers between devices, spread_all(): return lax.all_to_all(copies, axis, 0, 0)  6.34 us
    all_to_all x1, starting transfers between devices, trade(): return lax.all_to_all(blocks, axis, 0, 0, axis_index_groups=groups)  4.06 us
    ppermute x1, starting transfers between devices, per_device(): second_map = lax.ppermute(group_map_weight, 'head', second_move)  3.62 us
  transfers between devices with their start and end apart: 4, of which 2 were waited for; matrix products, arithmetic and copies ran while one was open for 4% of the time, Pallas kernels for 0%

profile of v2, /device:TPU:2, one launch (start us, length us, event | category | flops | bytes accessed | tf_op | source)
XLA Modules:
  0.0 145.7 jit_solution(13866726178737333632)
XLA Ops:
  0.7 3.6 %collective-permute-start.1 = (bf16[256,128]{1,0:T(8,128)(2,1)}, bf16[256,128]{1,0:T(8,128)(2,1)S(1)}, u32[]{:S(2)}, u32[]{:S(2)}) collective-permute-start(bf16[256,128]{1,0:T(8,128)(2,1)} %param.26), channel_id=1, source_target_pairs={{8,0},{0,1},{9,2},{1,3},{10,4},{2,5},{11,6},{3,7},{12,8},{4,9},{13... | collective-permute-start | bytes 196616 | tf_op jit(solution)/shard_map/ppermute | solution.py:84
  4.4 1.5 %collective-permute-start = (bf16[256,128]{1,0:T(8,128)(2,1)}, bf16[256,128]{1,0:T(8,128)(2,1)S(1)}, u32[]{:S(2)}, u32[]{:S(2)}) collective-permute-start(bf16[256,128]{1,0:T(8,128)(2,1)} %param.26), channel_id=1, source_target_pairs={{0,0},{8,1},{1,2},{9,3},{2,4},{10,5},{3,6},{11,7},{4,8},{12,9},{5,... | collective-permute-start | bytes 196616 | tf_op jit(solution)/shard_map/ppermute | solution.py:83
  5.9 1.3 broadcast_in_dim.66
  7.2 12.7 %all-to-all-start = ((bf16[16,8,256]{2,1,0:T(8,128)(2,1)}), bf16[16,8,256]{2,1,0:T(8,128)(2,1)S(1)}, u32[]{:S(2)}, u32[]{:S(2)}) async-start(bf16[16,8,256]{2,1,0:T(8,128)(2,1)} %broadcast_in_dim.66), calls=%async_computation | async-start | bytes 131072 | tf_op jit(solution)/shard_map/all_to_all | solution.py:35
  20.0 0.7 convert_reduce_fusion.4
  20.8 1.0 copy.76
  21.8 1.0 copy.64
  23.6 6.3 %all-to-all-done = bf16[16,8,256]{2,1,0:T(8,128)(2,1)S(1)} async-done(((bf16[16,8,256]{2,1,0:T(8,128)(2,1)}), bf16[16,8,256]{2,1,0:T(8,128)(2,1)S(1)}, u32[]{:S(2)}, u32[]{:S(2)}) %all-to-all-start) | async-done | bytes 65568 | tf_op jit(solution)/shard_map/all_to_all | solution.py:35
  30.1 0.2 fusion.20
  30.3 0.3 convolution_convert_fusion
  30.6 0.1 fusion
  30.9 26.1 %all_to_all.40 = bf16[32,4,1408]{2,1,0:T(4,128)(2,1)S(1)} all-to-all(bf16[32,4,1408]{2,1,0:T(4,128)(2,1)S(1)} %reshape.232), channel_id=1, replica_groups=mesh['dp'=32,'head'=16] {'dp'}, dimensions={0} | all-to-all | bytes 720896 | tf_op jit(solution)/shard_map/all_to_all | solution.py:39
  57.0 0.2 convert_reduce_fusion
  57.1 0.2 fusion.37
  57.7 0.2 fusion.38
  58.2 0.7 multiply_reduce_fusion
  59.4 13.3 %all_to_all.41 = bf16[32,4,640]{2,1,0:T(4,128)(2,1)S(1)} all-to-all(bf16[32,4,640]{2,1,0:T(4,128)(2,1)S(1)} %broadcast_in_dim.137), channel_id=1, replica_groups=mesh['dp'=32,'head'=16] {'dp'}, dimensions={0} | all-to-all | bytes 327680 | tf_op jit(solution)/shard_map/all_to_all | solution.py:35
  72.7 0.2 fusion.10
  73.0 0.2 fusion.14
  73.2 8.2 %all_to_all.42 = bf16[4,32,384]{2,1,0:T(8,128)(2,1)S(1)} all-to-all(bf16[4,32,384]{2,1,0:T(8,128)(2,1)S(1)} %bitcast.61), channel_id=1, replica_groups={{0,1,2,3},{4,5,6,7},{8,9,10,11},{12,13,14,15},{16,17,18,19},{20,21,22,2..., dimensions={0} | all-to-all | bytes 196608 | tf_op jit(solution)/shard_map/all_to_all | solution.py:39
  81.4 0.2 fusion.13
  81.8 14.9 %all_to_all.43 = bf16[16,32,256]{2,1,0:T(8,128)(2,1)S(1)} all-to-all(bf16[16,32,256]{2,1,0:T(8,128)(2,1)S(1)} %broadcast_in_dim.138), channel_id=1, replica_groups=mesh['dp'=32,'head'=16] {'head'}, dimensions={0} | all-to-all | bytes 524288 | tf_op jit(solution)/shard_map/all_to_all | solution.py:35
  97.1 0.2 convolution_convert_fusion.1
  97.4 16.7 %all_to_all.44 = bf16[32,4,1152]{2,1,0:T(4,128)(2,1)S(1)} all-to-all(bf16[32,4,1152]{2,1,0:T(4,128)(2,1)S(1)} %reshape.241), channel_id=1, replica_groups=mesh['dp'=32,'head'=16] {'dp'}, dimensions={0} | all-to-all | bytes 589824 | tf_op jit(solution)/shard_map/all_to_all | solution.py:39
  114.2 0.1 convert_reduce_fusion.1
  114.3 0.2 fusion.33
  114.7 15.4 %all_to_all.45 = bf16[32,4,1024]{2,1,0:T(4,128)(2,1)S(1)} all-to-all(bf16[32,4,1024]{2,1,0:T(4,128)(2,1)S(1)} %broadcast_in_dim.139), channel_id=1, replica_groups=mesh['dp'=32,'head'=16] {'dp'}, dimensions={0} | all-to-all | bytes 524288 | tf_op jit(solution)/shard_map/all_to_all | solution.py:35
  130.1 0.9 convolution_convert_fusion.2
  131.0 4.1 %all-to-all-start.7 = ((bf16[16,8,256]{2,1,0:T(8,128)(2,1)}), bf16[16,8,256]{2,1,0:T(8,128)(2,1)S(1)}, u32[]{:S(2)}, u32[]{:S(2)}) async-start(bf16[16,8,256]{2,1,0:T(8,128)(2,1)} %bitcast.20), calls=%async_computation.7 | async-start | bytes 131072 | tf_op jit(solution)/shard_map/all_to_all | solution.py:39
  135.1 1.3 select_bitcast_fusion
  136.5 8.6 %all-to-all-done.7 = bf16[16,8,256]{2,1,0:T(8,128)(2,1)S(1)} async-done(((bf16[16,8,256]{2,1,0:T(8,128)(2,1)}), bf16[16,8,256]{2,1,0:T(8,128)(2,1)S(1)}, u32[]{:S(2)}, u32[]{:S(2)}) %all-to-all-start.7) | async-done | bytes 65568 | tf_op jit(solution)/shard_map/all_to_all | solution.py:39
  145.1 0.6 add_convert_fusion.1
  (108 shorter events, 3.3 us)
Async XLA Ops:
  0.6 96.4 %copy-start = (bf16[256,1024]{1,0:T(8,128)(2,1)S(1)}, bf16[256,1024]{1,0:T(8,128)(2,1)}, u32[]{:S(2)}) copy-start(bf16[256,1024]{1,0:T(8,128)(2,1)} %param.38) | copy-start | bytes 1572868
  0.6 22.2 %copy-start.13 = (s32[4]{0:T(128)S(1)}, s32[4]{0:T(128)}, u32[]{:S(2)}) copy-start(s32[4]{0:T(128)} %param.40) | copy-start | bytes 52
  0.7 22.2 %copy-start.14 = (bf16[256]{0:T(256)(128)(2,1)S(1)}, bf16[256]{0:T(256)(128)(2,1)}, u32[]{:S(2)}) copy-start(bf16[256]{0:T(256)(128)(2,1)} %param.23) | copy-start | bytes 1540
  0.7 22.2 %copy-start.15 = (bf16[256]{0:T(256)(128)(2,1)S(1)}, bf16[256]{0:T(256)(128)(2,1)}, u32[]{:S(2)}) copy-start(bf16[256]{0:T(256)(128)(2,1)} %param.37) | copy-start | bytes 1540
  0.7 22.2 %copy-start.10 = (f32[8]{0:T(128)S(1)}, f32[8]{0:T(128)}, u32[]{:S(2)}) copy-start(f32[8]{0:T(128)} %param.30) | copy-start | bytes 100
  0.7 22.4 %copy-start.9 = (bf16[512]{0:T(512)(128)(2,1)S(1)}, bf16[512]{0:T(512)(128)(2,1)}, u32[]{:S(2)}) copy-start(bf16[512]{0:T(512)(128)(2,1)} %param.31) | copy-start | bytes 3076
  0.7 22.5 %copy-start.3 = (bf16[512,256]{1,0:T(8,128)(2,1)S(1)}, bf16[512,256]{1,0:T(8,128)(2,1)}, u32[]{:S(2)}) copy-start(bf16[512,256]{1,0:T(8,128)(2,1)} %param.32) | copy-start | bytes 786436
  0.7 22.7 %copy-start.8 = (bf16[256,8]{0,1:T(8,128)(2,1)S(1)}, bf16[256,8]{0,1:T(8,128)(2,1)}, u32[]{:S(2)}) copy-start(bf16[256,8]{0,1:T(8,128)(2,1)} %param.27) | copy-start | bytes 12292
  0.7 22.6 %copy-start.6 = (bf16[8,256,16]{1,2,0:T(8,128)(2,1)S(1)}, bf16[8,256,16]{1,2,0:T(8,128)(2,1)}, u32[]{:S(2)}) copy-start(bf16[8,256,16]{1,2,0:T(8,128)(2,1)} %param.33) | copy-start | bytes 196612
  0.7 22.8 %collective-permute-start.1 = (bf16[256,128]{1,0:T(8,128)(2,1)}, bf16[256,128]{1,0:T(8,128)(2,1)S(1)}, u32[]{:S(2)}, u32[]{:S(2)}) collective-permute-start(bf16[256,128]{1,0:T(8,128)(2,1)} %param.26), channel_id=1, source_target_pairs={{8,0},{0,1},{9,2},{1,3},{10,4},{2,5},{11,6},{3,7},{12,8},{4,9},{13... | collective-permute-start | bytes 196616 | tf_op jit(solution)/shard_map/ppermute | solution.py:84
  4.4 19.1 %collective-permute-start = (bf16[256,128]{1,0:T(8,128)(2,1)}, bf16[256,128]{1,0:T(8,128)(2,1)S(1)}, u32[]{:S(2)}, u32[]{:S(2)}) collective-permute-start(bf16[256,128]{1,0:T(8,128)(2,1)} %param.26), channel_id=1, source_target_pairs={{0,0},{8,1},{1,2},{9,3},{2,4},{10,5},{3,6},{11,7},{4,8},{12,9},{5,... | collective-permute-start | bytes 196616 | tf_op jit(solution)/shard_map/ppermute | solution.py:83
  7.2 16.3 %copy-start.4 = (bf16[256,512]{1,0:T(8,128)(2,1)S(1)}, bf16[256,512]{1,0:T(8,128)(2,1)}, u32[]{:S(2)}) copy-start(bf16[256,512]{1,0:T(8,128)(2,1)} %param.25) | copy-start | bytes 786436
  7.2 16.3 %copy-start.5 = (bf16[256,512]{1,0:T(8,128)(2,1)S(1)}, bf16[256,512]{1,0:T(8,128)(2,1)}, u32[]{:S(2)}) copy-start(bf16[256,512]{1,0:T(8,128)(2,1)} %param.24) | copy-start | bytes 786436
  7.2 22.8 %all-to-all-start = ((bf16[16,8,256]{2,1,0:T(8,128)(2,1)}), bf16[16,8,256]{2,1,0:T(8,128)(2,1)S(1)}, u32[]{:S(2)}, u32[]{:S(2)}) async-start(bf16[16,8,256]{2,1,0:T(8,128)(2,1)} %broadcast_in_dim.66), calls=%async_computation | async-start | bytes 131072 | tf_op jit(solution)/shard_map/all_to_all | solution.py:35
  30.8 27.1 %copy-start.11 = (f32[8]{0:T(128)S(1)}, f32[8]{0:T(128)}, u32[]{:S(2)}) copy-start(f32[8]{0:T(128)} %param.29) | copy-start | bytes 100
  30.8 27.1 %copy-start.12 = (f32[8]{0:T(128)S(1)}, f32[8]{0:T(128)}, u32[]{:S(2)}) copy-start(f32[8]{0:T(128)} %param.28) | copy-start | bytes 100
  30.9 27.3 %copy-start.1 = (f32[4,8,8192]{2,1,0:T(8,128)S(1)}, f32[4,8,8192]{2,1,0:T(8,128)}, u32[]{:S(2)}) copy-start(f32[4,8,8192]{2,1,0:T(8,128)} %param.22) | copy-start | bytes 3145732
  58.9 14.1 %copy-start.7 = (bf16[8,16,256]{2,1,0:T(8,128)(2,1)S(1)}, bf16[8,16,256]{2,1,0:T(8,128)(2,1)}, u32[]{:S(2)}) copy-start(bf16[8,16,256]{2,1,0:T(8,128)(2,1)} %param.36) | copy-start | bytes 196612
  97.4 32.7 %copy-start.2 = (bf16[1024,256]{1,0:T(8,128)(2,1)S(1)}, bf16[1024,256]{1,0:T(8,128)(2,1)}, u32[]{:S(2)}) copy-start(bf16[1024,256]{1,0:T(8,128)(2,1)} %param.39) | copy-start | bytes 1572868
  131.0 14.1 %all-to-all-start.7 = ((bf16[16,8,256]{2,1,0:T(8,128)(2,1)}), bf16[16,8,256]{2,1,0:T(8,128)(2,1)S(1)}, u32[]{:S(2)}, u32[]{:S(2)}) async-start(bf16[16,8,256]{2,1,0:T(8,128)(2,1)} %bitcast.20), calls=%async_computation.7 | async-start | bytes 131072 | tf_op jit(solution)/shard_map/all_to_all | solution.py:39

commit v3 on v2

--- a/solution.py
+++ b/solution.py
@@ -214,12 +214,13 @@
     x_heads = jax.nn.silu(x_part).reshape(own_rows, heads_here, HEAD_CHANNELS)
     old_state = state.reshape(own_rows, heads_here, HEAD_CHANNELS, NSTATE)
     step_x = step_size[:, :, None] * x_heads
-    fresh = (
-        forget[:, :, None, None] * old_state + step_x[:, :, :, None] * input_mat[:, None, None, :]
-    )
-    read_out = (
-        jnp.sum(fresh * output_mat[:, None, None, :], axis=3).reshape(own_rows, inner)
-        + skip_gain * x_heads.reshape(own_rows, inner)
+    maps_product = jnp.sum(input_mat * output_mat, axis=1)[:, None, None]
+    read_heads = (
+        forget[:, :, None] * jnp.sum(old_state * output_mat[:, None, None, :], axis=3)
+        + step_x * maps_product
+    )
+    read_out = read_heads.reshape(own_rows, inner) + skip_gain * x_heads.reshape(
+        own_rows, inner
     )
     gated = read_out * jax.nn.silu(z_part)
     gate_squares = jnp.sum(gated * gated, axis=1, keepdims=True)

time: 146 us -> 147 us (level)
  blocking collectives: 94.5 us -> 79.2 us
  waiting for transfers between devices: 14.9 us -> 27 us
  starting transfers between devices: 21.9 us -> 25.7 us
    all_to_all x3 -> x2, blocking collectives: 43.5 us -> 28.2 us  [spread_all(): return lax.all_to_all(copies, axis, 0, 0)]
    all_to_all x1 -> x2, waiting for transfers between devices: 6.34 us -> 18.4 us  [spread_all(): return lax.all_to_all(copies, axis, 0, 0)]
    all_to_all x1 -> x2, starting transfers between devices: 12.7 us -> 16.6 us  [spread_all(): return lax.all_to_all(copies, axis, 0, 0)]
  transfers between devices with their start and end apart: 4 -> 5, of which waited for: 2 -> 3; matrix products, arithmetic and copies ran while one was open for 4% -> 4% of each run, Pallas kernels for 0% -> 0%
where the time goes in v3:
time: 147 us
  blocking collectives  79.2 us (54%)
  waiting for transfers between devices  27 us (18%)
  starting transfers between devices  25.7 us (17%)
  other arithmetic  5.81 us (4%)
  local copies, waits for them, and re-layouts  5.6 us (4%)
  matrix products  2.22 us (2%)
    all_to_all x3, blocking collectives, trade(): return lax.all_to_all(blocks, axis, 0, 0, axis_index_groups=groups)  51 us
    all_to_all x2, blocking collectives, spread_all(): return lax.all_to_all(copies, axis, 0, 0)  28.2 us
    all_to_all x2, waiting for transfers between devices, spread_all(): return lax.all_to_all(copies, axis, 0, 0)  18.4 us
    all_to_all x2, starting transfers between devices, spread_all(): return lax.all_to_all(copies, axis, 0, 0)  16.6 us
    all_to_all x1, waiting for transfers between devices, trade(): return lax.all_to_all(blocks, axis, 0, 0, axis_index_groups=groups)  8.6 us
    all_to_all x1, starting transfers between devices, trade(): return lax.all_to_all(blocks, axis, 0, 0, axis_index_groups=groups)  3.98 us
    ppermute x1, starting transfers between devices, per_device(): second_map = lax.ppermute(group_map_weight, 'head', second_move)  3.62 us
  transfers between devices with their start and end apart: 5, of which 3 were waited for; matrix products, arithmetic and copies ran while one was open for 4% of the time, Pallas kernels for 0%

profile of v3, /device:TPU:2, one launch (start us, length us, event | category | flops | bytes accessed | tf_op | source)
XLA Modules:
  0.0 146.7 jit_solution(1577054659468067185)
XLA Ops:
  0.7 3.6 %collective-permute-start.1 = (bf16[256,128]{1,0:T(8,128)(2,1)}, bf16[256,128]{1,0:T(8,128)(2,1)S(1)}, u32[]{:S(2)}, u32[]{:S(2)}) collective-permute-start(bf16[256,128]{1,0:T(8,128)(2,1)} %param.26), channel_id=1, source_target_pairs={{8,0},{0,1},{9,2},{1,3},{10,4},{2,5},{11,6},{3,7},{12,8},{4,9},{13... | collective-permute-start | bytes 196616 | tf_op jit(solution)/shard_map/ppermute | solution.py:84
  4.4 1.5 %collective-permute-start = (bf16[256,128]{1,0:T(8,128)(2,1)}, bf16[256,128]{1,0:T(8,128)(2,1)S(1)}, u32[]{:S(2)}, u32[]{:S(2)}) collective-permute-start(bf16[256,128]{1,0:T(8,128)(2,1)} %param.26), channel_id=1, source_target_pairs={{0,0},{8,1},{1,2},{9,3},{2,4},{10,5},{3,6},{11,7},{4,8},{12,9},{5,... | collective-permute-start | bytes 196616 | tf_op jit(solution)/shard_map/ppermute | solution.py:83
  5.9 1.3 broadcast_in_dim.66
  7.2 12.7 %all-to-all-start = ((bf16[16,8,256]{2,1,0:T(8,128)(2,1)}), bf16[16,8,256]{2,1,0:T(8,128)(2,1)S(1)}, u32[]{:S(2)}, u32[]{:S(2)}) async-start(bf16[16,8,256]{2,1,0:T(8,128)(2,1)} %broadcast_in_dim.66), calls=%async_computation | async-start | bytes 131072 | tf_op jit(solution)/shard_map/all_to_all | solution.py:35
  20.0 0.7 convert_reduce_fusion.4
  20.8 1.0 copy.70
  21.8 1.0 copy.59
  23.6 6.3 %all-to-all-done = bf16[16,8,256]{2,1,0:T(8,128)(2,1)S(1)} async-done(((bf16[16,8,256]{2,1,0:T(8,128)(2,1)}), bf16[16,8,256]{2,1,0:T(8,128)(2,1)S(1)}, u32[]{:S(2)}, u32[]{:S(2)}) %all-to-all-start) | async-done | bytes 65568 | tf_op jit(solution)/shard_map/all_to_all | solution.py:35
  30.1 0.2 fusion.20
  30.3 0.3 convolution_convert_fusion
  30.9 26.1 %all_to_all.40 = bf16[32,4,1408]{2,1,0:T(4,128)(2,1)S(1)} all-to-all(bf16[32,4,1408]{2,1,0:T(4,128)(2,1)S(1)} %reshape.229), channel_id=1, replica_groups=mesh['dp'=32,'head'=16] {'dp'}, dimensions={0} | all-to-all | bytes 720896 | tf_op jit(solution)/shard_map/all_to_all | solution.py:39
  56.9 0.2 convert_reduce_fusion
  57.1 0.2 fusion.37
  57.6 0.2 fusion.38
  57.9 0.3 multiply_reduce_fusion
  59.1 13.3 %all_to_all.41 = bf16[32,4,640]{2,1,0:T(4,128)(2,1)S(1)} all-to-all(bf16[32,4,640]{2,1,0:T(4,128)(2,1)S(1)} %broadcast_in_dim.136), channel_id=1, replica_groups=mesh['dp'=32,'head'=16] {'dp'}, dimensions={0} | all-to-all | bytes 327680 | tf_op jit(solution)/shard_map/all_to_all | solution.py:35
  72.4 0.2 fusion.10
  72.7 0.2 fusion.14
  72.9 8.2 %all_to_all.42 = bf16[4,32,384]{2,1,0:T(8,128)(2,1)S(1)} all-to-all(bf16[4,32,384]{2,1,0:T(8,128)(2,1)S(1)} %bitcast.61), channel_id=1, replica_groups={{0,1,2,3},{4,5,6,7},{8,9,10,11},{12,13,14,15},{16,17,18,19},{20,21,22,2..., dimensions={0} | all-to-all | bytes 196608 | tf_op jit(solution)/shard_map/all_to_all | solution.py:39
  81.2 0.2 fusion.13
  81.5 14.9 %all_to_all.43 = bf16[16,32,256]{2,1,0:T(8,128)(2,1)S(1)} all-to-all(bf16[16,32,256]{2,1,0:T(8,128)(2,1)S(1)} %broadcast_in_dim.137), channel_id=1, replica_groups=mesh['dp'=32,'head'=16] {'head'}, dimensions={0} | all-to-all | bytes 524288 | tf_op jit(solution)/shard_map/all_to_all | solution.py:35
  96.8 0.2 convolution_convert_fusion.1
  97.2 16.7 %all_to_all.44 = bf16[32,4,1152]{2,1,0:T(4,128)(2,1)S(1)} all-to-all(bf16[32,4,1152]{2,1,0:T(4,128)(2,1)S(1)} %reshape.236), channel_id=1, replica_groups=mesh['dp'=32,'head'=16] {'dp'}, dimensions={0} | all-to-all | bytes 589824 | tf_op jit(solution)/shard_map/all_to_all | solution.py:39
  114.0 0.2 fusion.33
  114.3 0.8 broadcast_in_dim.138
  115.1 3.9 %all-to-all-start.6 = ((bf16[32,4,1024]{2,1,0:T(4,128)(2,1)}), bf16[32,4,1024]{2,1,0:T(4,128)(2,1)S(1)}, u32[]{:S(2)}, u32[]{:S(2)}) async-start(bf16[32,4,1024]{2,1,0:T(4,128)(2,1)} %broadcast_in_dim.138), calls=%async_computation.6 | async-start | bytes 524288 | tf_op jit(solution)/shard_map/all_to_all | solution.py:35
  119.1 12.0 %all-to-all-done.6 = bf16[32,4,1024]{2,1,0:T(4,128)(2,1)S(1)} async-done(((bf16[32,4,1024]{2,1,0:T(4,128)(2,1)}), bf16[32,4,1024]{2,1,0:T(4,128)(2,1)S(1)}, u32[]{:S(2)}, u32[]{:S(2)}) %all-to-all-start.6) | async-done | bytes 262176 | tf_op jit(solution)/shard_map/all_to_all | solution.py:35
  131.2 0.9 convolution_convert_fusion.2
  132.1 4.0 %all-to-all-start.7 = ((bf16[16,8,256]{2,1,0:T(8,128)(2,1)}), bf16[16,8,256]{2,1,0:T(8,128)(2,1)S(1)}, u32[]{:S(2)}, u32[]{:S(2)}) async-start(bf16[16,8,256]{2,1,0:T(8,128)(2,1)} %bitcast.20), calls=%async_computation.7 | async-start | bytes 131072 | tf_op jit(solution)/shard_map/all_to_all | solution.py:39
  136.2 1.3 select_bitcast_fusion
  137.5 8.6 %all-to-all-done.7 = bf16[16,8,256]{2,1,0:T(8,128)(2,1)S(1)} async-done(((bf16[16,8,256]{2,1,0:T(8,128)(2,1)}), bf16[16,8,256]{2,1,0:T(8,128)(2,1)S(1)}, u32[]{:S(2)}, u32[]{:S(2)}) %all-to-all-start.7) | async-done | bytes 65568 | tf_op jit(solution)/shard_map/all_to_all | solution.py:39
  146.1 0.6 add_convert_fusion.1
  (110 shorter events, 3.7 us)
Async XLA Ops:
  0.6 96.2 %copy-start = (bf16[256,1024]{1,0:T(8,128)(2,1)S(1)}, bf16[256,1024]{1,0:T(8,128)(2,1)}, u32[]{:S(2)}) copy-start(bf16[256,1024]{1,0:T(8,128)(2,1)} %param.38) | copy-start | bytes 1572868
  0.6 22.2 %copy-start.13 = (s32[4]{0:T(128)S(1)}, s32[4]{0:T(128)}, u32[]{:S(2)}) copy-start(s32[4]{0:T(128)} %param.40) | copy-start | bytes 52
  0.7 22.2 %copy-start.14 = (bf16[256]{0:T(256)(128)(2,1)S(1)}, bf16[256]{0:T(256)(128)(2,1)}, u32[]{:S(2)}) copy-start(bf16[256]{0:T(256)(128)(2,1)} %param.23) | copy-start | bytes 1540
  0.7 22.2 %copy-start.15 = (bf16[256]{0:T(256)(128)(2,1)S(1)}, bf16[256]{0:T(256)(128)(2,1)}, u32[]{:S(2)}) copy-start(bf16[256]{0:T(256)(128)(2,1)} %param.37) | copy-start | bytes 1540
  0.7 22.2 %copy-start.10 = (f32[8]{0:T(128)S(1)}, f32[8]{0:T(128)}, u32[]{:S(2)}) copy-start(f32[8]{0:T(128)} %param.30) | copy-start | bytes 100
  0.7 22.4 %copy-start.9 = (bf16[512]{0:T(512)(128)(2,1)S(1)}, bf16[512]{0:T(512)(128)(2,1)}, u32[]{:S(2)}) copy-start(bf16[512]{0:T(512)(128)(2,1)} %param.31) | copy-start | bytes 3076
  0.7 22.5 %copy-start.3 = (bf16[512,256]{1,0:T(8,128)(2,1)S(1)}, bf16[512,256]{1,0:T(8,128)(2,1)}, u32[]{:S(2)}) copy-start(bf16[512,256]{1,0:T(8,128)(2,1)} %param.32) | copy-start | bytes 786436
  0.7 22.7 %copy-start.8 = (bf16[256,8]{0,1:T(8,128)(2,1)S(1)}, bf16[256,8]{0,1:T(8,128)(2,1)}, u32[]{:S(2)}) copy-start(bf16[256,8]{0,1:T(8,128)(2,1)} %param.27) | copy-start | bytes 12292
  0.7 22.6 %copy-start.6 = (bf16[8,256,16]{1,2,0:T(8,128)(2,1)S(1)}, bf16[8,256,16]{1,2,0:T(8,128)(2,1)}, u32[]{:S(2)}) copy-start(bf16[8,256,16]{1,2,0:T(8,128)(2,1)} %param.33) | copy-start | bytes 196612
  0.7 22.8 %collective-permute-start.1 = (bf16[256,128]{1,0:T(8,128)(2,1)}, bf16[256,128]{1,0:T(8,128)(2,1)S(1)}, u32[]{:S(2)}, u32[]{:S(2)}) collective-permute-start(bf16[256,128]{1,0:T(8,128)(2,1)} %param.26), channel_id=1, source_target_pairs={{8,0},{0,1},{9,2},{1,3},{10,4},{2,5},{11,6},{3,7},{12,8},{4,9},{13... | collective-permute-start | bytes 196616 | tf_op jit(solution)/shard_map/ppermute | solution.py:84
  4.4 19.1 %collective-permute-start = (bf16[256,128]{1,0:T(8,128)(2,1)}, bf16[256,128]{1,0:T(8,128)(2,1)S(1)}, u32[]{:S(2)}, u32[]{:S(2)}) collective-permute-start(bf16[256,128]{1,0:T(8,128)(2,1)} %param.26), channel_id=1, source_target_pairs={{0,0},{8,1},{1,2},{9,3},{2,4},{10,5},{3,6},{11,7},{4,8},{12,9},{5,... | collective-permute-start | bytes 196616 | tf_op jit(solution)/shard_map/ppermute | solution.py:83
  7.2 16.3 %copy-start.4 = (bf16[256,512]{1,0:T(8,128)(2,1)S(1)}, bf16[256,512]{1,0:T(8,128)(2,1)}, u32[]{:S(2)}) copy-start(bf16[256,512]{1,0:T(8,128)(2,1)} %param.25) | copy-start | bytes 786436
  7.2 16.3 %copy-start.5 = (bf16[256,512]{1,0:T(8,128)(2,1)S(1)}, bf16[256,512]{1,0:T(8,128)(2,1)}, u32[]{:S(2)}) copy-start(bf16[256,512]{1,0:T(8,128)(2,1)} %param.24) | copy-start | bytes 786436
  7.2 22.8 %all-to-all-start = ((bf16[16,8,256]{2,1,0:T(8,128)(2,1)}), bf16[16,8,256]{2,1,0:T(8,128)(2,1)S(1)}, u32[]{:S(2)}, u32[]{:S(2)}) async-start(bf16[16,8,256]{2,1,0:T(8,128)(2,1)} %broadcast_in_dim.66), calls=%async_computation | async-start | bytes 131072 | tf_op jit(solution)/shard_map/all_to_all | solution.py:35
  30.8 27.1 %copy-start.1 = (f32[4,8,8192]{2,1,0:T(8,128)S(1)}, f32[4,8,8192]{2,1,0:T(8,128)}, u32[]{:S(2)}) copy-start(f32[4,8,8192]{2,1,0:T(8,128)} %param.22) | copy-start | bytes 3145732
  56.9 1.4 copy-start.11
  56.9 1.4 copy-start.12
  58.4 14.3 %copy-start.7 = (bf16[8,16,256]{2,1,0:T(8,128)(2,1)S(1)}, bf16[8,16,256]{2,1,0:T(8,128)(2,1)}, u32[]{:S(2)}) copy-start(bf16[8,16,256]{2,1,0:T(8,128)(2,1)} %param.36) | copy-start | bytes 196612
  97.2 34.1 %copy-start.2 = (bf16[1024,256]{1,0:T(8,128)(2,1)S(1)}, bf16[1024,256]{1,0:T(8,128)(2,1)}, u32[]{:S(2)}) copy-start(bf16[1024,256]{1,0:T(8,128)(2,1)} %param.39) | copy-start | bytes 1572868
  115.1 16.1 %all-to-all-start.6 = ((bf16[32,4,1024]{2,1,0:T(4,128)(2,1)}), bf16[32,4,1024]{2,1,0:T(4,128)(2,1)S(1)}, u32[]{:S(2)}, u32[]{:S(2)}) async-start(bf16[32,4,1024]{2,1,0:T(4,128)(2,1)} %broadcast_in_dim.138), calls=%async_computation.6 | async-start | bytes 524288 | tf_op jit(solution)/shard_map/all_to_all | solution.py:35
  132.1 14.0 %all-to-all-start.7 = ((bf16[16,8,256]{2,1,0:T(8,128)(2,1)}), bf16[16,8,256]{2,1,0:T(8,128)(2,1)S(1)}, u32[]{:S(2)}, u32[]{:S(2)}) async-start(bf16[16,8,256]{2,1,0:T(8,128)(2,1)} %bitcast.20), calls=%async_computation.7 | async-start | bytes 131072 | tf_op jit(solution)/shard_map/all_to_all | solution.py:39

commit v4 on v3

--- a/solution.py
+++ b/solution.py
@@ -227,9 +227,10 @@
     mixed = (gated * live_inner).astype(bf16)
     gate_high = lax.reduce_precision(gate_squares, exponent_bits=8, mantissa_bits=7)
     gate_tail = (gate_high * pick_first + (gate_squares - gate_high) * pick_second).astype(bf16)
-    mixed_all = spread_all(
-        jnp.concatenate([mixed, gate_tail], axis=1), "dp", dp_count
-    ).reshape(all_rows, inner + LANES)
+    mixed_sent, forget, step_x, input_mat = lax.optimization_barrier(
+        (jnp.concatenate([mixed, gate_tail], axis=1), forget, step_x, input_mat)
+    )
+    mixed_all = spread_all(mixed_sent, "dp", dp_count).reshape(all_rows, inner + LANES)
 
     mixed_main = jnp.dot(mixed_all[:, :inner], joined_out, preferred_element_type=f32)
     low_out = mixed_main[:, local_width:] * lane_pick.astype(f32)

time: 147 us -> 146 us (level)
  blocking collectives: 79.2 us -> 94.5 us
  waiting for transfers between devices: 27 us -> 14.9 us
  starting transfers between devices: 25.7 us -> 21.9 us
    all_to_all x2 -> x3, blocking collectives: 28.2 us -> 43.5 us  [spread_all(): return lax.all_to_all(copies, axis, 0, 0)]
    all_to_all x2 -> x1, waiting for transfers between devices: 18.4 us -> 6.34 us  [spread_all(): return lax.all_to_all(copies, axis, 0, 0)]
    all_to_all x2 -> x1, starting transfers between devices: 16.6 us -> 12.7 us  [spread_all(): return lax.all_to_all(copies, axis, 0, 0)]
  transfers between devices with their start and end apart: 5 -> 4, of which waited for: 3 -> 2; matrix products, arithmetic and copies ran while one was open for 4% -> 4% of each run, Pallas kernels for 0% -> 0%
where the time goes in v4:
time: 146 us
  blocking collectives  94.5 us (65%)
  starting transfers between devices  21.9 us (15%)
  waiting for transfers between devices  14.9 us (10%)
  other arithmetic  5.8 us (4%)
  local copies, waits for them, and re-layouts  4.89 us (3%)
  matrix products  2.22 us (2%)
    all_to_all x3, blocking collectives, trade(): return lax.all_to_all(blocks, axis, 0, 0, axis_index_groups=groups)  51 us
    all_to_all x3, blocking collectives, spread_all(): return lax.all_to_all(copies, axis, 0, 0)  43.5 us
    all_to_all x1, starting transfers between devices, spread_all(): return lax.all_to_all(copies, axis, 0, 0)  12.7 us
    all_to_all x1, waiting for transfers between devices, trade(): return lax.all_to_all(blocks, axis, 0, 0, axis_index_groups=groups)  8.6 us
    all_to_all x1, waiting for transfers between devices, spread_all(): return lax.all_to_all(copies, axis, 0, 0)  6.34 us
    all_to_all x1, starting transfers between devices, trade(): return lax.all_to_all(blocks, axis, 0, 0, axis_index_groups=groups)  4.07 us
    ppermute x1, starting transfers between devices, per_device(): second_map = lax.ppermute(group_map_weight, 'head', second_move)  3.62 us
  transfers between devices with their start and end apart: 4, of which 2 were waited for; matrix products, arithmetic and copies ran while one was open for 4% of the time, Pallas kernels for 0%

profile of v4, /device:TPU:2, one launch (start us, length us, event | category | flops | bytes accessed | tf_op | source)
XLA Modules:
  0.0 145.6 jit_solution(6957990365745345600)
XLA Ops:
  0.7 3.6 %collective-permute-start.1 = (bf16[256,128]{1,0:T(8,128)(2,1)}, bf16[256,128]{1,0:T(8,128)(2,1)S(1)}, u32[]{:S(2)}, u32[]{:S(2)}) collective-permute-start(bf16[256,128]{1,0:T(8,128)(2,1)} %param.26), channel_id=1, source_target_pairs={{8,0},{0,1},{9,2},{1,3},{10,4},{2,5},{11,6},{3,7},{12,8},{4,9},{13... | collective-permute-start | bytes 196616 | tf_op jit(solution)/shard_map/ppermute | solution.py:84
  4.4 1.5 %collective-permute-start = (bf16[256,128]{1,0:T(8,128)(2,1)}, bf16[256,128]{1,0:T(8,128)(2,1)S(1)}, u32[]{:S(2)}, u32[]{:S(2)}) collective-permute-start(bf16[256,128]{1,0:T(8,128)(2,1)} %param.26), channel_id=1, source_target_pairs={{0,0},{8,1},{1,2},{9,3},{2,4},{10,5},{3,6},{11,7},{4,8},{12,9},{5,... | collective-permute-start | bytes 196616 | tf_op jit(solution)/shard_map/ppermute | solution.py:83
  5.9 1.3 broadcast_in_dim.66
  7.2 12.7 %all-to-all-start = ((bf16[16,8,256]{2,1,0:T(8,128)(2,1)}), bf16[16,8,256]{2,1,0:T(8,128)(2,1)S(1)}, u32[]{:S(2)}, u32[]{:S(2)}) async-start(bf16[16,8,256]{2,1,0:T(8,128)(2,1)} %broadcast_in_dim.66), calls=%async_computation | async-start | bytes 131072 | tf_op jit(solution)/shard_map/all_to_all | solution.py:35
  20.0 0.7 convert_reduce_fusion.4
  20.8 1.0 copy.70
  21.8 1.0 copy.59
  23.6 6.3 %all-to-all-done = bf16[16,8,256]{2,1,0:T(8,128)(2,1)S(1)} async-done(((bf16[16,8,256]{2,1,0:T(8,128)(2,1)}), bf16[16,8,256]{2,1,0:T(8,128)(2,1)S(1)}, u32[]{:S(2)}, u32[]{:S(2)}) %all-to-all-start) | async-done | bytes 65568 | tf_op jit(solution)/shard_map/all_to_all | solution.py:35
  30.1 0.2 fusion.20
  30.3 0.3 convolution_convert_fusion
  30.6 0.1 fusion
  30.9 26.1 %all_to_all.40 = bf16[32,4,1408]{2,1,0:T(4,128)(2,1)S(1)} all-to-all(bf16[32,4,1408]{2,1,0:T(4,128)(2,1)S(1)} %reshape.229), channel_id=1, replica_groups=mesh['dp'=32,'head'=16] {'dp'}, dimensions={0} | all-to-all | bytes 720896 | tf_op jit(solution)/shard_map/all_to_all | solution.py:39
  56.9 0.2 convert_reduce_fusion
  57.1 0.2 fusion.37
  57.6 0.2 fusion.38
  57.9 0.3 multiply_reduce_fusion
  59.3 13.3 %all_to_all.41 = bf16[32,4,640]{2,1,0:T(4,128)(2,1)S(1)} all-to-all(bf16[32,4,640]{2,1,0:T(4,128)(2,1)S(1)} %broadcast_in_dim.136), channel_id=1, replica_groups=mesh['dp'=32,'head'=16] {'dp'}, dimensions={0} | all-to-all | bytes 327680 | tf_op jit(solution)/shard_map/all_to_all | solution.py:35
  72.6 0.2 fusion.10
  72.8 0.2 fusion.14
  73.1 8.2 %all_to_all.42 = bf16[4,32,384]{2,1,0:T(8,128)(2,1)S(1)} all-to-all(bf16[4,32,384]{2,1,0:T(8,128)(2,1)S(1)} %bitcast.61), channel_id=1, replica_groups={{0,1,2,3},{4,5,6,7},{8,9,10,11},{12,13,14,15},{16,17,18,19},{20,21,22,2..., dimensions={0} | all-to-all | bytes 196608 | tf_op jit(solution)/shard_map/all_to_all | solution.py:39
  81.3 0.2 fusion.13
  81.6 14.9 %all_to_all.43 = bf16[16,32,256]{2,1,0:T(8,128)(2,1)S(1)} all-to-all(bf16[16,32,256]{2,1,0:T(8,128)(2,1)S(1)} %broadcast_in_dim.137), channel_id=1, replica_groups=mesh['dp'=32,'head'=16] {'head'}, dimensions={0} | all-to-all | bytes 524288 | tf_op jit(solution)/shard_map/all_to_all | solution.py:35
  96.9 0.2 convolution_convert_fusion.1
  97.3 16.7 %all_to_all.44 = bf16[32,4,1152]{2,1,0:T(4,128)(2,1)S(1)} all-to-all(bf16[32,4,1152]{2,1,0:T(4,128)(2,1)S(1)} %reshape.237), channel_id=1, replica_groups=mesh['dp'=32,'head'=16] {'dp'}, dimensions={0} | all-to-all | bytes 589824 | tf_op jit(solution)/shard_map/all_to_all | solution.py:39
  114.0 0.1 convert_reduce_fusion.1
  114.2 0.2 fusion.33
  114.5 15.4 %all_to_all.45 = bf16[32,4,1024]{2,1,0:T(4,128)(2,1)S(1)} all-to-all(bf16[32,4,1024]{2,1,0:T(4,128)(2,1)S(1)} %broadcast_in_dim.138), channel_id=1, replica_groups=mesh['dp'=32,'head'=16] {'dp'}, dimensions={0} | all-to-all | bytes 524288 | tf_op jit(solution)/shard_map/all_to_all | solution.py:35
  130.0 0.9 convolution_convert_fusion.2
  130.8 4.1 %all-to-all-start.7 = ((bf16[16,8,256]{2,1,0:T(8,128)(2,1)}), bf16[16,8,256]{2,1,0:T(8,128)(2,1)S(1)}, u32[]{:S(2)}, u32[]{:S(2)}) async-start(bf16[16,8,256]{2,1,0:T(8,128)(2,1)} %bitcast.20), calls=%async_computation.7 | async-start | bytes 131072 | tf_op jit(solution)/shard_map/all_to_all | solution.py:39
  135.0 1.3 select_bitcast_fusion
  136.3 8.6 %all-to-all-done.7 = bf16[16,8,256]{2,1,0:T(8,128)(2,1)S(1)} async-done(((bf16[16,8,256]{2,1,0:T(8,128)(2,1)}), bf16[16,8,256]{2,1,0:T(8,128)(2,1)S(1)}, u32[]{:S(2)}, u32[]{:S(2)}) %all-to-all-start.7) | async-done | bytes 65568 | tf_op jit(solution)/shard_map/all_to_all | solution.py:39
  145.0 0.6 add_convert_fusion.1
  (109 shorter events, 3.5 us)
Async XLA Ops:
  0.6 96.3 %copy-start = (bf16[256,1024]{1,0:T(8,128)(2,1)S(1)}, bf16[256,1024]{1,0:T(8,128)(2,1)}, u32[]{:S(2)}) copy-start(bf16[256,1024]{1,0:T(8,128)(2,1)} %param.38) | copy-start | bytes 1572868
  0.6 22.2 %copy-start.13 = (s32[4]{0:T(128)S(1)}, s32[4]{0:T(128)}, u32[]{:S(2)}) copy-start(s32[4]{0:T(128)} %param.40) | copy-start | bytes 52
  0.7 22.2 %copy-start.14 = (bf16[256]{0:T(256)(128)(2,1)S(1)}, bf16[256]{0:T(256)(128)(2,1)}, u32[]{:S(2)}) copy-start(bf16[256]{0:T(256)(128)(2,1)} %param.23) | copy-start | bytes 1540
  0.7 22.2 %copy-start.15 = (bf16[256]{0:T(256)(128)(2,1)S(1)}, bf16[256]{0:T(256)(128)(2,1)}, u32[]{:S(2)}) copy-start(bf16[256]{0:T(256)(128)(2,1)} %param.37) | copy-start | bytes 1540
  0.7 22.2 %copy-start.10 = (f32[8]{0:T(128)S(1)}, f32[8]{0:T(128)}, u32[]{:S(2)}) copy-start(f32[8]{0:T(128)} %param.30) | copy-start | bytes 100
  0.7 22.4 %copy-start.9 = (bf16[512]{0:T(512)(128)(2,1)S(1)}, bf16[512]{0:T(512)(128)(2,1)}, u32[]{:S(2)}) copy-start(bf16[512]{0:T(512)(128)(2,1)} %param.31) | copy-start | bytes 3076
  0.7 22.5 %copy-start.3 = (bf16[512,256]{1,0:T(8,128)(2,1)S(1)}, bf16[512,256]{1,0:T(8,128)(2,1)}, u32[]{:S(2)}) copy-start(bf16[512,256]{1,0:T(8,128)(2,1)} %param.32) | copy-start | bytes 786436
  0.7 22.7 %copy-start.8 = (bf16[256,8]{0,1:T(8,128)(2,1)S(1)}, bf16[256,8]{0,1:T(8,128)(2,1)}, u32[]{:S(2)}) copy-start(bf16[256,8]{0,1:T(8,128)(2,1)} %param.27) | copy-start | bytes 12292
  0.7 22.6 %copy-start.6 = (bf16[8,256,16]{1,2,0:T(8,128)(2,1)S(1)}, bf16[8,256,16]{1,2,0:T(8,128)(2,1)}, u32[]{:S(2)}) copy-start(bf16[8,256,16]{1,2,0:T(8,128)(2,1)} %param.33) | copy-start | bytes 196612
  0.7 22.8 %collective-permute-start.1 = (bf16[256,128]{1,0:T(8,128)(2,1)}, bf16[256,128]{1,0:T(8,128)(2,1)S(1)}, u32[]{:S(2)}, u32[]{:S(2)}) collective-permute-start(bf16[256,128]{1,0:T(8,128)(2,1)} %param.26), channel_id=1, source_target_pairs={{8,0},{0,1},{9,2},{1,3},{10,4},{2,5},{11,6},{3,7},{12,8},{4,9},{13... | collective-permute-start | bytes 196616 | tf_op jit(solution)/shard_map/ppermute | solution.py:84
  4.4 19.1 %collective-permute-start = (bf16[256,128]{1,0:T(8,128)(2,1)}, bf16[256,128]{1,0:T(8,128)(2,1)S(1)}, u32[]{:S(2)}, u32[]{:S(2)}) collective-permute-start(bf16[256,128]{1,0:T(8,128)(2,1)} %param.26), channel_id=1, source_target_pairs={{0,0},{8,1},{1,2},{9,3},{2,4},{10,5},{3,6},{11,7},{4,8},{12,9},{5,... | collective-permute-start | bytes 196616 | tf_op jit(solution)/shard_map/ppermute | solution.py:83
  7.2 16.3 %copy-start.4 = (bf16[256,512]{1,0:T(8,128)(2,1)S(1)}, bf16[256,512]{1,0:T(8,128)(2,1)}, u32[]{:S(2)}) copy-start(bf16[256,512]{1,0:T(8,128)(2,1)} %param.25) | copy-start | bytes 786436
  7.2 16.3 %copy-start.5 = (bf16[256,512]{1,0:T(8,128)(2,1)S(1)}, bf16[256,512]{1,0:T(8,128)(2,1)}, u32[]{:S(2)}) copy-start(bf16[256,512]{1,0:T(8,128)(2,1)} %param.24) | copy-start | bytes 786436
  7.2 22.8 %all-to-all-start = ((bf16[16,8,256]{2,1,0:T(8,128)(2,1)}), bf16[16,8,256]{2,1,0:T(8,128)(2,1)S(1)}, u32[]{:S(2)}, u32[]{:S(2)}) async-start(bf16[16,8,256]{2,1,0:T(8,128)(2,1)} %broadcast_in_dim.66), calls=%async_computation | async-start | bytes 131072 | tf_op jit(solution)/shard_map/all_to_all | solution.py:35
  30.8 27.1 %copy-start.1 = (f32[4,8,8192]{2,1,0:T(8,128)S(1)}, f32[4,8,8192]{2,1,0:T(8,128)}, u32[]{:S(2)}) copy-start(f32[4,8,8192]{2,1,0:T(8,128)} %param.22) | copy-start | bytes 3145732
  56.9 1.4 copy-start.11
  56.9 1.4 copy-start.12
  58.5 14.3 %copy-start.7 = (bf16[8,16,256]{2,1,0:T(8,128)(2,1)S(1)}, bf16[8,16,256]{2,1,0:T(8,128)(2,1)}, u32[]{:S(2)}) copy-start(bf16[8,16,256]{2,1,0:T(8,128)(2,1)} %param.36) | copy-start | bytes 196612
  97.3 32.7 %copy-start.2 = (bf16[1024,256]{1,0:T(8,128)(2,1)S(1)}, bf16[1024,256]{1,0:T(8,128)(2,1)}, u32[]{:S(2)}) copy-start(bf16[1024,256]{1,0:T(8,128)(2,1)} %param.39) | copy-start | bytes 1572868
  130.8 14.1 %all-to-all-start.7 = ((bf16[16,8,256]{2,1,0:T(8,128)(2,1)}), bf16[16,8,256]{2,1,0:T(8,128)(2,1)S(1)}, u32[]{:S(2)}, u32[]{:S(2)}) async-start(bf16[16,8,256]{2,1,0:T(8,128)(2,1)} %bitcast.20), calls=%async_computation.7 | async-start | bytes 131072 | tf_op jit(solution)/shard_map/all_to_all | solution.py:39
